TPU v7x, 32 devices: a whole 2x2x4 slice. The times are simulated.
32 devices in a mesh: lon: 8 (over y, x, core), lat: 4 (over z).
Axes of the slice: x: 2, y: 2, z: 4, core: 2. Of those that a mesh axis runs over, the one named last changes fastest.
Arguments:
- fields: bfloat16 [4, 192, 896, 80], P(None, 'lat', 'lon'), may hold values from -6 to 6
- lift_weight: bfloat16 [80, 128], replicated, may hold values from -0.625 to 0.625
- near_kernel: bfloat16 [3, 3, 128, 128], replicated, may hold values from -0.1875 to 0.1875
- far_kernel: bfloat16 [3, 3, 128, 128], replicated, may hold values from -0.1875 to 0.1875
- mix_weight: bfloat16 [128, 128], replicated, may hold values from -0.5 to 0.5
Outputs:
- result: bfloat16 [4, 192, 896, 128], P(None, 'lat', 'lon')
All inputs are finite; a program needn't handle non-finite values.
Results may differ from a plain program's by a relative error of at most 0.0067.
Values may be sent and summed in bfloat16 or wider, within the bound.
No kernel may reach another device: no remote copies, remote signals or barrier semaphores. Data moves between devices by JAX's collectives and lax.ppermute only.
A program may use at most 256 MiB of HBM per device.

v0:
```python
import jax
import jax.numpy as jnp
from jax import lax
from jax.sharding import PartitionSpec as P

FAR = 4


def padded_2(block, sides, width, periodic):
    for axis, dim in sides:
        count = lax.axis_size(axis)
        forward = [(i, i + 1) for i in range(count - 1)]
        if periodic:
            forward.append((count - 1, 0))
        backward = [(target, source) for source, target in forward]
        low = lax.ppermute(
            lax.slice_in_dim(block, block.shape[dim] - width, None, axis=dim), axis, forward
        )
        high = lax.ppermute(lax.slice_in_dim(block, 0, width, axis=dim), axis, backward)
        block = jnp.concatenate([low, block, high], axis=dim)
    return block


def passed_along(block, axis, distance):
    devices = range(lax.axis_size(axis))
    route = [((i - distance) % len(devices), i) for i in devices]
    return lax.ppermute(block, axis, route)


def convolve(padded, kernel, step, rows, cols):
    total = jnp.zeros((padded.shape[0], rows, cols, kernel.shape[3]), jnp.float32)
    for row_tap in range(3):
        for col_tap in range(3):
            piece = padded[
                :, row_tap * step : row_tap * step + rows, col_tap * step : col_tap * step + cols
            ]
            total = total + jnp.einsum(
                "bhwc,cd->bhwd", piece, kernel[row_tap, col_tap], preferred_element_type=jnp.float32
            )
    return total


def edge_rows(field, width):
    return jnp.concatenate([field[:, :width][:, ::-1], field[:, -width:][:, ::-1]], axis=1)


def place_poles(padded, received, margin, width):
    inner = padded.shape[1] - 2 * margin
    north = lax.axis_index("lat") == 0
    south = lax.axis_index("lat") == lax.axis_size("lat") - 1
    top = jnp.where(north, received[:, :width], padded[:, margin - width : margin])
    bottom = jnp.where(
        south, received[:, width:], padded[:, margin + inner : margin + inner + width]
    )
    return jnp.concatenate(
        [
            padded[:, : margin - width],
            top,
            padded[:, margin : margin + inner],
            bottom,
            padded[:, margin + inner + width :],
        ],
        axis=1,
    )


def on_device(fields, lift_weight, near_kernel, far_kernel, mix_weight):
    rows = fields.shape[1]
    cols = fields.shape[2]
    half = lax.axis_size("lon") // 2
    lifted = jnp.einsum(
        "bhwc,cd->bhwd", fields, lift_weight, preferred_element_type=jnp.float32
    ).astype(jnp.bfloat16)
    banded = padded_2(lifted, (("lat", 1),), 1, False)
    received = passed_along(edge_rows(lifted, 1), "lon", half)
    banded = place_poles(banded, received, 1, 1)
    padded = padded_2(banded, (("lon", 2),), 1, True)
    first = jax.nn.silu(convolve(padded, near_kernel, 1, rows, cols)).astype(jnp.bfloat16)
    banded = padded_2(first, (("lat", 1),), FAR, False)
    received = passed_along(edge_rows(first, FAR), "lon", half)
    banded = place_poles(banded, received, FAR, FAR)
    widened = padded_2(banded, (("lon", 2),), FAR, True)
    second = jax.nn.silu(convolve(widened, far_kernel, FAR, rows, cols)).astype(jnp.bfloat16)
    mixed = jnp.einsum("bhwc,cd->bhwd", second, mix_weight, preferred_element_type=jnp.float32)
    return mixed.astype(jnp.bfloat16)


def solution(mesh):
    return jax.shard_map(
        on_device,
        mesh=mesh,
        in_specs=(P(None, "lat", "lon", None), P(), P(), P(), P()),
        out_specs=P(None, "lat", "lon", None),
        check_vma=False,
    )
```

profile of v0, /device:TPU:0, one launch (start us, length us, event | category | flops | bytes accessed | tf_op | source)
XLA Modules:
  0.0 207.3 jit_solution(18131460275153172567)
XLA Ops:
  3.8 5.1 %collective-permute-start.1 = (bf16[4,1,112,128]{3,2,1,0:T(8,128)(2,1)S(1)}, bf16[4,1,112,128]{3,2,1,0:T(8,128)(2,1)S(1)}, u32[]{:S(2)}, u32[]{:S(2)}) collective-permute-start(bf16[4,1,112,128]{3,2,1,0:T(8,128)(2,1)S(1)} %get-tuple-element.15), channel_id=1, source_target_pairs={{0,1},{1,2},{2,3},{4,5},{5,6},{6,7},{8,9},{9,10},{10,11},{12,13},{... | collective-permute-start | bytes 344072 | tf_op jit(solution)/shard_map/ppermute | solution.py:16
  11.8 5.7 %fusion.61 = f32[4,48,112,128]{3,2,1,0:T(8,128)} fusion(bf16[4,48,112,128]{3,2,1,0:T(8,128)(2,1)S(1)} %convolution_convert_fusion, bf16[3,3,128,128]{3,2,1,0:T(8,128)(2,1)} %param.7), kind=kOutput, calls=%fused_computation.76 | convolution fusion | flops 704643072 | bytes 16547840 | tf_op jit(solution)/shard_map/bhwc,cd->bhwd/dot_general | solution.py:37
  17.6 8.5 %fusion.12 = f32[4,48,112,128]{3,2,1,0:T(8,128)} fusion(bf16[4,1,112,128]{3,2,1,0:T(8,128)(2,1)S(1)} %get-tuple-element.20, bf16[4,48,112,128]{3,2,1,0:T(8,128)(2,1)} %copy-done.1, bf16[3,3,128,128]{3,2,1,0:T(8,128)(2,1)S(1)} %copy-done.3), kind=kOutput, calls=%fused_computation.18 | convolution fusion | flops 715882496 | bytes 16662528 | tf_op jit(solution)/shard_map/bhwc,cd->bhwd/dot_general | solution.py:37
  26.8 4.9 %fusion.8 = f32[4,48,112,128]{3,2,1,0:T(8,128)} fusion(bf16[4,48,112,128]{3,2,1,0:T(8,128)(2,1)S(1)} %bitcast.143, bf16[4,1,112,128]{3,2,1,0:T(8,128)(2,1)S(1)} %get-tuple-element.19, bf16[3,3,128,128]{3,2,1,0:T(8,128)(2,1)S(1)} %copy-done.3), kind=kOutput, calls=%fused_computation.14 | convolution fusion | flops 715882496 | bytes 16662528 | tf_op jit(solution)/shard_map/bhwc,cd->bhwd/dot_general | solution.py:37
  32.3 7.3 %pad_maximum_fusion.1 = (bf16[4,50,113,128]{3,2,1,0:T(8,128)(2,1)S(1)}, bf16[4,50,113,128]{3,2,1,0:T(8,128)(2,1)S(1)}) fusion(bf16[4,50,1,128]{3,2,1,0:T(2,128)(2,1)S(1)} %collective-permute-done.4, bf16[4,1,112,128]{3,2,1,0:T(8,128)(2,1)S(1)} %get-tuple-element.20, bf16[4,48,112,128]{3,2,1,0:T(8,128)(2,1)S(1)} %bitcast.143, ...), kind=kLoop, calls=%fused_computation.5 | loop fusion | flops 46284800 | bytes 17408000 | tf_op jit(solution)/shard_map/concatenate | solution.py:20
  39.7 5.3 %fusion.30 = f32[4,48,112,128]{3,2,1,0:T(8,128)} fusion(bf16[4,50,113,128]{3,2,1,0:T(8,128)(2,1)S(1)} %get-tuple-element.10, bf16[3,3,128,128]{3,2,1,0:T(8,128)(2,1)S(1)} %copy-done.3), kind=kOutput, calls=%fused_computation.36 | convolution fusion | flops 704643072 | bytes 16547840 | tf_op jit(solution)/shard_map/bhwc,cd->bhwd/dot_general | solution.py:37
  45.0 5.0 %fusion.34 = f32[4,48,112,128]{3,2,1,0:T(8,128)} fusion(bf16[4,50,113,128]{3,2,1,0:T(8,128)(2,1)S(1)} %get-tuple-element.10, bf16[3,3,128,128]{3,2,1,0:T(8,128)(2,1)S(1)} %copy-done.3), kind=kOutput, calls=%fused_computation.40 | convolution fusion | flops 704643072 | bytes 16547840 | tf_op jit(solution)/shard_map/bhwc,cd->bhwd/dot_general | solution.py:37
  49.9 4.9 %fusion.32 = f32[4,48,112,128]{3,2,1,0:T(8,128)} fusion(bf16[4,50,113,128]{3,2,1,0:T(8,128)(2,1)S(1)} %get-tuple-element.9, bf16[3,3,128,128]{3,2,1,0:T(8,128)(2,1)S(1)} %copy-done.3), kind=kOutput, calls=%fused_computation.38 | convolution fusion | flops 704643072 | bytes 16547840 | tf_op jit(solution)/shard_map/bhwc,cd->bhwd/dot_general | solution.py:37
  54.8 4.9 %fusion.36 = f32[4,48,112,128]{3,2,1,0:T(8,128)} fusion(bf16[4,50,113,128]{3,2,1,0:T(8,128)(2,1)S(1)} %get-tuple-element.9, bf16[3,3,128,128]{3,2,1,0:T(8,128)(2,1)S(1)} %copy-done.3), kind=kOutput, calls=%fused_computation.42 | convolution fusion | flops 704643072 | bytes 16547840 | tf_op jit(solution)/shard_map/bhwc,cd->bhwd/dot_general | solution.py:37
  59.7 5.0 %fusion.38 = f32[4,48,112,128]{3,2,1,0:T(8,128)} fusion(bf16[4,50,113,128]{3,2,1,0:T(8,128)(2,1)S(1)} %get-tuple-element.10, bf16[3,3,128,128]{3,2,1,0:T(8,128)(2,1)S(1)} %copy-done.3), kind=kOutput, calls=%fused_computation.44 | convolution fusion | flops 704643072 | bytes 16547840 | tf_op jit(solution)/shard_map/bhwc,cd->bhwd/dot_general | solution.py:37
  64.7 32.2 %multiply_convert_fusion.1 = bf16[4,48,112,128]{3,2,1,0:T(8,128)(2,1)} fusion(f32[4,48,112,128]{3,2,1,0:T(8,128)} %fusion.12, f32[4,48,112,128]{3,2,1,0:T(8,128)} %fusion.30, f32[4,48,112,128]{3,2,1,0:T(8,128)} %fusion.32, f32[4,48,112,128]{3,2,1,0:T(8,128)} %fusion.61, f32[4,48,112,128]{3,2,1,0:T(8,128)} %fusion.34, f32[4,48,112,128]{3,2,1,0:T(8,128)} %fusion.36, ...), kind=kOutput, calls=%fused_computation.1 | convolution fusion | flops 740425728 | bytes 99123200 | tf_op jit(solution)/shard_map/bhwc,cd->bhwd/dot_general | solution.py:37
  99.3 4.6 %collective-permute-start.6 = (bf16[4,4,112,128]{3,2,1,0:T(8,128)(2,1)S(1)}, bf16[4,4,112,128]{3,2,1,0:T(8,128)(2,1)S(1)}, u32[]{:S(2)}, u32[]{:S(2)}) collective-permute-start(bf16[4,4,112,128]{3,2,1,0:T(8,128)(2,1)S(1)} %get-tuple-element.13), channel_id=1, source_target_pairs={{0,1},{1,2},{2,3},{4,5},{5,6},{6,7},{8,9},{9,10},{10,11},{12,13},{... | collective-permute-start | bytes 1376264 | tf_op jit(solution)/shard_map/ppermute | solution.py:16
  105.2 9.4 %collective-permute-done.6 = bf16[4,4,112,128]{3,2,1,0:T(8,128)(2,1)S(1)} collective-permute-done((bf16[4,4,112,128]{3,2,1,0:T(8,128)(2,1)S(1)}, bf16[4,4,112,128]{3,2,1,0:T(8,128)(2,1)S(1)}, u32[]{:S(2)}, u32[]{:S(2)}) %collective-permute-start.6) | collective-permute-done | bytes 458784 | tf_op jit(solution)/shard_map/ppermute | solution.py:16
  114.6 4.1 %collective-permute-done.7 = bf16[4,4,112,128]{3,2,1,0:T(8,128)(2,1)S(1)} collective-permute-done((bf16[4,4,112,128]{3,2,1,0:T(8,128)(2,1)S(1)}, bf16[4,4,112,128]{3,2,1,0:T(8,128)(2,1)S(1)}, u32[]{:S(2)}, u32[]{:S(2)}) %collective-permute-start.7) | collective-permute-done | bytes 458784 | tf_op jit(solution)/shard_map/ppermute | solution.py:19
  125.7 4.9 %fusion.4 = f32[4,48,112,128]{3,2,1,0:T(8,128)} fusion(bf16[4,4,112,128]{3,2,1,0:T(8,128)(2,1)S(1)} %get-tuple-element.18, bf16[4,48,112,128]{3,2,1,0:T(8,128)(2,1)S(1)} %bitcast.141, bf16[3,3,128,128]{3,2,1,0:T(8,128)(2,1)S(1)} %copy-done.4), kind=kOutput, calls=%fused_computation.10 | convolution fusion | flops 716570624 | bytes 17006592 | tf_op jit(solution)/shard_map/bhwc,cd->bhwd/dot_general | solution.py:37
  130.6 4.9 %fusion = f32[4,48,112,128]{3,2,1,0:T(8,128)} fusion(bf16[4,48,112,128]{3,2,1,0:T(8,128)(2,1)S(1)} %bitcast.141, bf16[4,4,112,128]{3,2,1,0:T(8,128)(2,1)S(1)} %get-tuple-element.17, bf16[3,3,128,128]{3,2,1,0:T(8,128)(2,1)S(1)} %copy-done.4), kind=kOutput, calls=%fused_computation.6 | convolution fusion | flops 716570624 | bytes 17006592 | tf_op jit(solution)/shard_map/bhwc,cd->bhwd/dot_general | solution.py:37
  135.5 10.0 %maximum_maximum_fusion = (bf16[4,56,116,128]{3,2,1,0:T(8,128)(2,1)S(1)}, bf16[4,56,116,128]{3,2,1,0:T(8,128)(2,1)S(1)}) fusion(bf16[4,4,112,128]{3,2,1,0:T(8,128)(2,1)S(1)} %get-tuple-element.18, bf16[4,48,112,128]{3,2,1,0:T(8,128)(2,1)S(1)} %bitcast.141, bf16[4,4,112,128]{3,2,1,0:T(8,128)(2,1)S(1)} %get-tuple-element.17, ...), kind=kLoop, calls=%fused_computation.2 | loop fusion | flops 53215232 | bytes 20185088 | tf_op jit(solution)/shard_map/concatenate | solution.py:20
  145.5 5.1 %fusion.16 = f32[4,48,112,128]{3,2,1,0:T(8,128)} fusion(bf16[4,56,116,128]{3,2,1,0:T(8,128)(2,1)S(1)} %get-tuple-element.6, bf16[3,3,128,128]{3,2,1,0:T(8,128)(2,1)S(1)} %copy-done.4), kind=kOutput, calls=%fused_computation.22 | convolution fusion | flops 704643072 | bytes 16547840 | tf_op jit(solution)/shard_map/bhwc,cd->bhwd/dot_general | solution.py:37
  150.6 5.0 %fusion.20 = f32[4,48,112,128]{3,2,1,0:T(8,128)} fusion(bf16[4,56,116,128]{3,2,1,0:T(8,128)(2,1)S(1)} %get-tuple-element.6, bf16[3,3,128,128]{3,2,1,0:T(8,128)(2,1)S(1)} %copy-done.4), kind=kOutput, calls=%fused_computation.26 | convolution fusion | flops 704643072 | bytes 16547840 | tf_op jit(solution)/shard_map/bhwc,cd->bhwd/dot_general | solution.py:37
  155.6 4.9 %fusion.18 = f32[4,48,112,128]{3,2,1,0:T(8,128)} fusion(bf16[4,56,116,128]{3,2,1,0:T(8,128)(2,1)S(1)} %get-tuple-element.5, bf16[3,3,128,128]{3,2,1,0:T(8,128)(2,1)S(1)} %copy-done.4), kind=kOutput, calls=%fused_computation.24 | convolution fusion | flops 704643072 | bytes 16547840 | tf_op jit(solution)/shard_map/bhwc,cd->bhwd/dot_general | solution.py:37
  160.4 5.0 %fusion.22 = f32[4,48,112,128]{3,2,1,0:T(8,128)} fusion(bf16[4,56,116,128]{3,2,1,0:T(8,128)(2,1)S(1)} %get-tuple-element.5, bf16[3,3,128,128]{3,2,1,0:T(8,128)(2,1)S(1)} %copy-done.4), kind=kOutput, calls=%fused_computation.28 | convolution fusion | flops 704643072 | bytes 16547840 | tf_op jit(solution)/shard_map/bhwc,cd->bhwd/dot_general | solution.py:37
  165.4 4.9 %fusion.24 = f32[4,48,112,128]{3,2,1,0:T(8,128)} fusion(bf16[4,56,116,128]{3,2,1,0:T(8,128)(2,1)S(1)} %get-tuple-element.6, bf16[3,3,128,128]{3,2,1,0:T(8,128)(2,1)S(1)} %copy-done.4), kind=kOutput, calls=%fused_computation.30 | convolution fusion | flops 704643072 | bytes 16547840 | tf_op jit(solution)/shard_map/bhwc,cd->bhwd/dot_general | solution.py:37
  170.3 5.0 %fusion.26 = f32[4,48,112,128]{3,2,1,0:T(8,128)} fusion(bf16[4,56,116,128]{3,2,1,0:T(8,128)(2,1)S(1)} %get-tuple-element.5, bf16[3,3,128,128]{3,2,1,0:T(8,128)(2,1)S(1)} %copy-done.4), kind=kOutput, calls=%fused_computation.32 | convolution fusion | flops 704643072 | bytes 16547840 | tf_op jit(solution)/shard_map/bhwc,cd->bhwd/dot_general | solution.py:37
  175.3 32.0 %fusion.43 = bf16[4,48,112,128]{3,2,1,0:T(8,128)(2,1)} fusion(f32[4,48,112,128]{3,2,1,0:T(8,128)} %fusion.16, f32[4,48,112,128]{3,2,1,0:T(8,128)} %fusion.4, f32[4,48,112,128]{3,2,1,0:T(8,128)} %fusion.18, f32[4,48,112,128]{3,2,1,0:T(8,128)} %fusion.20, f32[4,48,112,128]{3,2,1,0:T(8,128)} %fusion.22, f32[4,48,112,128]{3,2,1,0:T(8,128)} %fusion.24, ...), kind=kOutput, calls=%fused_computation.48 | convolution fusion | flops 1447821312 | bytes 99155968 | tf_op jit(solution)/shard_map/bhwc,cd->bhwd/dot_general | solution.py:84
  (47 shorter events, 18.6 us)
Async XLA Ops:
  0.0 175.3 %copy-start = (bf16[128,128]{1,0:T(8,128)(2,1)S(1)}, bf16[128,128]{1,0:T(8,128)(2,1)}, u32[]{:S(2)}) copy-start(bf16[128,128]{1,0:T(8,128)(2,1)} %param.9) | copy-start | bytes 98308
  3.8 8.0 %copy-start.1 = (bf16[4,48,112,128]{3,2,1,0:T(8,128)(2,1)}, bf16[4,48,112,128]{3,2,1,0:T(8,128)(2,1)S(1)}, u32[]{:S(2)}) copy-start(bf16[4,48,112,128]{3,2,1,0:T(8,128)(2,1)S(1)} %convolution_convert_fusion) | copy-start | bytes 16515076
  3.8 13.8 %copy-start.3 = (bf16[3,3,128,128]{3,2,1,0:T(8,128)(2,1)S(1)}, bf16[3,3,128,128]{3,2,1,0:T(8,128)(2,1)}, u32[]{:S(2)}) copy-start(bf16[3,3,128,128]{3,2,1,0:T(8,128)(2,1)} %param.7) | copy-start | bytes 884740
  3.8 13.7 %collective-permute-start.1 = (bf16[4,1,112,128]{3,2,1,0:T(8,128)(2,1)S(1)}, bf16[4,1,112,128]{3,2,1,0:T(8,128)(2,1)S(1)}, u32[]{:S(2)}, u32[]{:S(2)}) collective-permute-start(bf16[4,1,112,128]{3,2,1,0:T(8,128)(2,1)S(1)} %get-tuple-element.15), channel_id=1, source_target_pairs={{0,1},{1,2},{2,3},{4,5},{5,6},{6,7},{8,9},{9,10},{10,11},{12,13},{... | collective-permute-start | bytes 344072 | tf_op jit(solution)/shard_map/ppermute | solution.py:16
  8.9 8.6 %collective-permute-start.2 = (bf16[4,1,112,128]{3,2,1,0:T(8,128)(2,1)S(1)}, bf16[4,1,112,128]{3,2,1,0:T(8,128)(2,1)S(1)}, u32[]{:S(2)}, u32[]{:S(2)}) collective-permute-start(bf16[4,1,112,128]{3,2,1,0:T(8,128)(2,1)S(1)} %get-tuple-element.16), channel_id=1, source_target_pairs={{1,0},{2,1},{3,2},{5,4},{6,5},{7,6},{9,8},{10,9},{11,10},{13,12},{... | collective-permute-start | bytes 344072 | tf_op jit(solution)/shard_map/ppermute | solution.py:19
  10.3 7.3 %collective-permute-start = (bf16[4,2,112,128]{3,2,1,0:T(8,128)(2,1)S(1)}, bf16[4,2,112,128]{3,2,1,0:T(8,128)(2,1)S(1)}, u32[]{:S(2)}, u32[]{:S(2)}) collective-permute-start(bf16[4,2,112,128]{3,2,1,0:T(8,128)(2,1)S(1)} %pad_maximum_fusion.6), channel_id=1, source_target_pairs={{16,0},{20,4},{24,8},{28,12},{0,16},{4,20},{8,24},{12,28},{17,1},{... | collective-permute-start | bytes 688136 | tf_op jit(solution)/shard_map/ppermute | solution.py:27
  17.6 8.5 %slice-start.2 = ((s8[5505024]{0:T(1024)(128)(4,1)}), s8[1310720]{0:T(1024)(128)(4,1)S(1)}, s32[]{:S(2)}) async-start(s8[5505024]{0:T(1024)(128)(4,1)} %bitcast.142), calls=%async_computation.2 | async-start | bytes 2621440
  17.6 8.5 %slice-start.3 = ((s8[5505024]{0:T(1024)(128)(4,1)}), s8[4194304]{0:T(1024)(128)(4,1)S(1)}, s32[]{:S(2)}) async-start(s8[5505024]{0:T(1024)(128)(4,1)} %bitcast.142), calls=%async_computation.3 | async-start | bytes 8388608
  26.3 5.5 %collective-permute-start.4 = (bf16[4,50,1,128]{3,2,1,0:T(2,128)(2,1)S(1)}, bf16[4,50,1,128]{3,2,1,0:T(2,128)(2,1)S(1)}, u32[]{:S(2)}, u32[]{:S(2)}) collective-permute-start(bf16[4,50,1,128]{3,2,1,0:T(2,128)(2,1)S(1)} %get-tuple-element.11), channel_id=1, source_target_pairs={{4,0},{8,4},{12,8},{16,12},{20,16},{24,20},{28,24},{0,28},{5,1},{9... | collective-permute-start | bytes 153608 | tf_op jit(solution)/shard_map/ppermute | solution.py:19
  26.8 5.5 %collective-permute-start.3 = (bf16[4,50,1,128]{3,2,1,0:T(2,128)(2,1)S(1)}, bf16[4,50,1,128]{3,2,1,0:T(2,128)(2,1)S(1)}, u32[]{:S(2)}, u32[]{:S(2)}) collective-permute-start(bf16[4,50,1,128]{3,2,1,0:T(2,128)(2,1)S(1)} %get-tuple-element.12), channel_id=1, source_target_pairs={{0,4},{4,8},{8,12},{12,16},{16,20},{20,24},{24,28},{28,0},{1,5},{5... | collective-permute-start | bytes 153608 | tf_op jit(solution)/shard_map/ppermute | solution.py:16
  39.6 15.2 %copy-start.2 = (bf16[4,50,113,128]{3,2,1,0:T(8,128)(2,1)}, bf16[4,50,113,128]{3,2,1,0:T(8,128)(2,1)S(1)}, u32[]{:S(2)}) copy-start(bf16[4,50,113,128]{3,2,1,0:T(8,128)(2,1)S(1)} %get-tuple-element.9) | copy-start | bytes 17356804
  96.9 28.8 %slice-start = ((s8[5505024]{0:T(1024)(128)(4,1)}), s8[1310720]{0:T(1024)(128)(4,1)S(1)}, s32[]{:S(2)}) async-start(s8[5505024]{0:T(1024)(128)(4,1)} %bitcast.140), calls=%async_computation | async-start | bytes 2621440
  96.9 28.8 %copy-start.4 = (bf16[3,3,128,128]{3,2,1,0:T(8,128)(2,1)S(1)}, bf16[3,3,128,128]{3,2,1,0:T(8,128)(2,1)}, u32[]{:S(2)}) copy-start(bf16[3,3,128,128]{3,2,1,0:T(8,128)(2,1)} %param.8) | copy-start | bytes 884740
  98.4 27.3 %slice-start.1 = ((s8[5505024]{0:T(1024)(128)(4,1)}), s8[4194304]{0:T(1024)(128)(4,1)S(1)}, s32[]{:S(2)}) async-start(s8[5505024]{0:T(1024)(128)(4,1)} %bitcast.140), calls=%async_computation.1 | async-start | bytes 8388608
  98.4 23.1 %collective-permute-start.5 = (bf16[4,8,112,128]{3,2,1,0:T(8,128)(2,1)S(1)}, bf16[4,8,112,128]{3,2,1,0:T(8,128)(2,1)S(1)}, u32[]{:S(2)}, u32[]{:S(2)}) collective-permute-start(bf16[4,8,112,128]{3,2,1,0:T(8,128)(2,1)S(1)} %pad_maximum_fusion.2), channel_id=1, source_target_pairs={{16,0},{20,4},{24,8},{28,12},{0,16},{4,20},{8,24},{12,28},{17,1},{... | collective-permute-start | bytes 2752520 | tf_op jit(solution)/shard_map/ppermute | solution.py:27
  99.3 15.3 %collective-permute-start.6 = (bf16[4,4,112,128]{3,2,1,0:T(8,128)(2,1)S(1)}, bf16[4,4,112,128]{3,2,1,0:T(8,128)(2,1)S(1)}, u32[]{:S(2)}, u32[]{:S(2)}) collective-permute-start(bf16[4,4,112,128]{3,2,1,0:T(8,128)(2,1)S(1)} %get-tuple-element.13), channel_id=1, source_target_pairs={{0,1},{1,2},{2,3},{4,5},{5,6},{6,7},{8,9},{9,10},{10,11},{12,13},{... | collective-permute-start | bytes 1376264 | tf_op jit(solution)/shard_map/ppermute | solution.py:16
  103.9 14.9 %collective-permute-start.7 = (bf16[4,4,112,128]{3,2,1,0:T(8,128)(2,1)S(1)}, bf16[4,4,112,128]{3,2,1,0:T(8,128)(2,1)S(1)}, u32[]{:S(2)}, u32[]{:S(2)}) collective-permute-start(bf16[4,4,112,128]{3,2,1,0:T(8,128)(2,1)S(1)} %get-tuple-element.14), channel_id=1, source_target_pairs={{1,0},{2,1},{3,2},{5,4},{6,5},{7,6},{9,8},{10,9},{11,10},{13,12},{... | collective-permute-start | bytes 1376264 | tf_op jit(solution)/shard_map/ppermute | solution.py:19
  123.0 12.6 %collective-permute-start.8 = (bf16[4,56,4,128]{3,2,1,0:T(4,128)(2,1)S(1)}, bf16[4,56,4,128]{3,2,1,0:T(4,128)(2,1)S(1)}, u32[]{:S(2)}, u32[]{:S(2)}) collective-permute-start(bf16[4,56,4,128]{3,2,1,0:T(4,128)(2,1)S(1)} %get-tuple-element.7), channel_id=1, source_target_pairs={{0,4},{4,8},{8,12},{12,16},{16,20},{20,24},{24,28},{28,0},{1,5},{5... | collective-permute-start | bytes 688136 | tf_op jit(solution)/shard_map/ppermute | solution.py:16
  123.0 12.5 %collective-permute-start.9 = (bf16[4,56,4,128]{3,2,1,0:T(4,128)(2,1)S(1)}, bf16[4,56,4,128]{3,2,1,0:T(4,128)(2,1)S(1)}, u32[]{:S(2)}, u32[]{:S(2)}) collective-permute-start(bf16[4,56,4,128]{3,2,1,0:T(4,128)(2,1)S(1)} %get-tuple-element.8), channel_id=1, source_target_pairs={{4,0},{8,4},{12,8},{16,12},{20,16},{24,20},{28,24},{0,28},{5,1},{9... | collective-permute-start | bytes 688136 | tf_op jit(solution)/shard_map/ppermute | solution.py:19
where the time goes:
time: 208 us; the launch traced here: 207 us
  matrix products  152 us (73%)
  other arithmetic  19 us (9%)
  starting transfers between devices  18 us (9%)
  waiting for transfers between devices  16.9 us (8%)
    dot_general x17, matrix products, convolve(): jnp.einsum('bhwc,cd->bhwd', piece, kernel[row_tap, col_tap], preferred_el...  116 us
    dot_general x1, matrix products, on_device(): jnp.einsum('bhwc,cd->bhwd', second, mix_weight, preferred_element_type=jn...  32 us
    concatenate x2, other arithmetic, padded_2(): block = jnp.concatenate([low, block, high], axis=dim)  17.3 us
    ppermute x4, waiting for transfers between devices, padded_2(): lax.ppermute(lax.slice_in_dim(block, block.shape[dim] - width, None, axis...  10 us
    ppermute x4, starting transfers between devices, padded_2(): lax.ppermute(lax.slice_in_dim(block, block.shape[dim] - width, None, axis...  9.72 us
    ppermute x4, starting transfers between devices, padded_2(): lax.ppermute(lax.slice_in_dim(block, 0, width, axis=dim), axis, backward)  5.76 us
  transfers between devices with their start and end apart: 10, of which 4 were waited for; matrix products, arithmetic and copies ran while one was open for 10% of the time, Pallas kernels for 0%

commit v1 on v0

v1 whole, which is shorter than its diff:
```python
import functools

import jax
import jax.numpy as jnp
from jax import lax
from jax.experimental import pallas as pl
from jax.experimental.pallas import tpu as pltpu
from jax.sharding import PartitionSpec as P

FAR = 4
BF = jnp.bfloat16
F32 = jnp.float32
HALO = 5
SLOT = 8
MIB = 1 << 20
INNER_MIB = 60
OUTER_MIB = 60


def dot(a, b):
    return jnp.dot(a, b, preferred_element_type=F32)


def silu_of_half(h):
    return h + h * jnp.tanh(h)


def with_columns(row, right, left):
    return jnp.concatenate([row, right, left], axis=1)


def slot(ref, lead, row):
    per = 128 // SLOT
    at = (row % per) * SLOT
    return ref[lead, row // per, :, at : at + SLOT]


def three_taps(row):
    before = jnp.concatenate([row[:, 127:], row[:, :127]], axis=1)
    after = jnp.concatenate([row[:, 1:], row[:, :1]], axis=1)
    fill = jnp.zeros((256 - 3 * row.shape[0], 128), BF)
    return jnp.concatenate([before, row, after, fill], axis=0).T


def pack_columns(x_ref, west_ref, east_ref):
    per = 128 // SLOT
    cols = x_ref.shape[3]
    for group in range(west_ref.shape[1]):
        rows = range(group * per, min((group + 1) * per, x_ref.shape[1]))
        west = [x_ref[0, r, :, 0:SLOT] for r in rows]
        east = [x_ref[0, r, :, cols - SLOT : cols] for r in rows]
        west_ref[0, group] = jnp.concatenate(west, axis=1)
        east_ref[0, group] = jnp.concatenate(east, axis=1)


def make_weights(lift_ref, near_ref, far_ref, mix_ref, wn_ref, wf_ref, wm_ref):
    cin, chan = lift_ref.shape
    wn_ref[...] = jnp.zeros_like(wn_ref)
    wf_ref[...] = jnp.zeros_like(wf_ref)
    wm_ref[...] = jnp.zeros_like(wm_ref)
    for a in range(3):
        for b in range(3):
            near = (0.5 * dot(lift_ref[...], near_ref[a, b])).astype(BF)
            far = (0.5 * far_ref[a, b].astype(F32)).astype(BF)
            for o in range(2):
                out = slice(o * chan, (o + 1) * chan)
                wn_ref[a + o, b * cin : (b + 1) * cin, out] = near
                k = a + o
                base = (2 * b + k // 2) * 256 + (k % 2) * chan
                wf_ref[base : base + chan, out] = far
    wm_ref[:chan, :chan] = mix_ref[...]
    wm_ref[chan:, chan:] = mix_ref[...]


def pack_rows(top_ref, bottom_ref, right_ref, left_ref, p_ref, q_ref):
    even = lax.rem(lax.axis_index("lat"), 2) == 0
    rows = right_ref.shape[1] * (128 // SLOT)
    batch = top_ref.shape[0]

    def write(first, second):
        for b in range(batch):
            for k in range(HALO):
                t = with_columns(top_ref[b, k], slot(right_ref, b, k), slot(left_ref, b, k))
                r = rows - HALO + k
                u = with_columns(
                    bottom_ref[b, 8 - HALO + k], slot(right_ref, b, r), slot(left_ref, b, r)
                )
                first[b, k] = t
                second[b, k] = u

    @pl.when(even)
    def _():
        write(p_ref, q_ref)

    @pl.when(jnp.logical_not(even))
    def _():
        write(q_ref, p_ref)


def spread(f2, at, piece):
    inner = f2.shape[-2]
    f2[(0, *at)] = jnp.concatenate([piece[128 - FAR :], piece[: inner - FAR]], axis=0)
    f2[(1, *at)] = piece[:inner]
    f2[(2, *at)] = piece[FAR : inner + FAR]


def near_block(rows, wn_ref):
    lhs = jnp.concatenate(
        [jnp.concatenate([pair[i] for pair in rows], axis=0) for i in range(4)], axis=1
    )
    h = dot(lhs, wn_ref[...].reshape(4 * 256, 256))
    return silu_of_half(h).astype(BF)


def far_block(f2, lead, g, wf_ref):
    lhs = jnp.concatenate(
        [
            jnp.concatenate([f2[(b, *lead, g + k, h, c)] for c in range(4)], axis=0)
            for b in range(3)
            for k in range(2)
            for h in range(2)
        ],
        axis=1,
    )
    return silu_of_half(dot(lhs, wf_ref[...])).astype(BF)


def halves(v, pair):
    return [v[128 * pair : 128 * pair + 128, 128 * o : 128 * o + 128] for o in range(2)]


def inner_rows(
    x_ref, right_ref, left_ref, lift_ref, near_ref, far_ref, mix_ref, out_ref, fx_ref,
    x3, f2, s, wn_ref, wf_ref, wm_ref,
):
    @pl.when(pl.program_id(0) == 0)
    def _():
        make_weights(lift_ref, near_ref, far_ref, mix_ref, wn_ref, wf_ref, wm_ref)

    blocks = f2.shape[1]
    cols = f2.shape[-2]
    low = FAR - 1
    for i in range(x3.shape[0]):
        r = i + low
        row = with_columns(x_ref[0, r], slot(right_ref, 0, r), slot(left_ref, 0, r))
        x3[i] = three_taps(row)
    for m in range(blocks):
        v = near_block(
            [[x3[8 * m + 2 * p + i] for i in range(4)] for p in range(4)], wn_ref
        )
        for p in range(4):
            for o, piece in enumerate(halves(v, p)):
                h, c = divmod(2 * p + o, 4)
                spread(f2, (m, h, c), piece)
                if m == 0:
                    fx_ref[0, 0, h, c] = piece
                if m == blocks - 1:
                    fx_ref[0, 1, h, c] = piece
    span = 4 * cols
    for g in range(blocks - 1):
        s[g * span : (g + 1) * span] = far_block(f2, (), g, wf_ref)
    y = dot(s[...], wm_ref[...]).astype(BF)
    for g in range(blocks - 1):
        for c in range(4):
            at = g * span + c * cols
            for h in range(2):
                out_ref[0, 8 * g + 4 * h + c] = y[at : at + cols, 128 * h : 128 * h + 128]


def outer_rows(
    top_ref, bottom_ref, right_ref, left_ref, p_ref, q_ref, fx_ref,
    lift_ref, near_ref, far_ref, mix_ref, _, out_ref,
    x3, f2, s, y, wn_ref, wf_ref, wm_ref, sems,
):
    make_weights(lift_ref, near_ref, far_ref, mix_ref, wn_ref, wf_ref, wm_ref)
    lat = lax.axis_index("lat")
    even = lax.rem(lat, 2) == 0
    poles = (lat == 0, lat == lax.axis_size("lat") - 1)
    cols = f2.shape[-2]
    total = right_ref.shape[1] * (128 // SLOT)
    span = 4 * cols
    units = [(b, side) for b in range(top_ref.shape[0]) for side in range(2)]
    for u, (b, side) in enumerate(units):
        pole = poles[side]
        moved = pole if side == 0 else jnp.logical_not(pole)
        from_p = even if side == 0 else jnp.logical_not(even)
        base = jnp.where(moved, 1, 0)
        close = jnp.where(moved, 0, HALO - 1)
        for k in range(HALO):
            taps = three_taps(jnp.where(from_p, p_ref[b, k], q_ref[b, k]))
            x3[u, base + k] = taps
        x3[u, 6 if side == 0 else 11] = x3[u, base + close]
        own = top_ref if side == 0 else bottom_ref
        for k in range(HALO):
            r = k if side == 0 else total - HALO + k
            t = k if side == 0 else 8 - HALO + k
            taps = three_taps(with_columns(own[b, t], slot(right_ref, b, r), slot(left_ref, b, r)))
            x3[u, (7 if side == 0 else 6) + k] = taps
            if k == (0 if side == 0 else HALO - 1):
                x3[u, jnp.where(moved, 0, HALO)] = taps
    for u, (b, side) in enumerate(units):
        pole = poles[side]
        v = near_block(
            [[x3[u, first + i] for i in range(4)] for first in (0, 2, 6, 8)], wn_ref
        )
        for q in range(2):
            for o, piece in enumerate(halves(v, q)):
                c = 2 * q + o
                spread(f2, (u, side, side, jnp.where(pole, 3 - c, c)), piece)
            for o, piece in enumerate(halves(v, 2 + q)):
                spread(f2, (u, side, 1 - side, 2 * q + o), piece)
        for h in range(2):
            for c in range(4):
                spread(f2, (u, 1 - side, h, c), fx_ref[b, side, h, c])
    for u in range(len(units)):
        s[u * span : (u + 1) * span] = far_block(f2, (u,), 0, wf_ref)
    copies = []
    for u, (b, side) in enumerate(units):
        done = dot(s[u * span : (u + 1) * span], wm_ref[...]).astype(BF)
        for c in range(4):
            for h in range(2):
                y[u, 4 * h + c] = done[cols * c : cols * c + cols, 128 * h : 128 * h + 128]
        to = out_ref.at[b, pl.ds(0 if side == 0 else total - 8, 8)]
        copy = pltpu.make_async_copy(y.at[u], to, sems.at[u])
        copy.start()
        copies.append(copy)
    for copy in copies:
        copy.wait()


def whole(shape):
    return pl.BlockSpec(shape, lambda *_: (0,) * len(shape))


def per_sample(shape):
    return pl.BlockSpec((1,) + shape[1:], lambda b, *_: (b,) + (0,) * (len(shape) - 1))


def params(mib):
    return pltpu.CompilerParams(vmem_limit_bytes=mib * MIB)


def cost(flops, nbytes):
    return pl.CostEstimate(flops=flops, bytes_accessed=nbytes, transcendentals=0)


def swaps(lats, lons, offset):
    half = lons // 2
    pairs = []
    for lat in range(lats):
        other = lat + (1 if (lat + offset) % 2 == 0 else -1)
        for lon in range(lons):
            if 0 <= other < lats:
                pairs.append((lon * lats + other, lon * lats + lat))
            else:
                pairs.append(((lon + half) % lons * lats + lat, lon * lats + lat))
    return pairs


def on_device(fields, lift_weight, near_kernel, far_kernel, mix_weight):
    batch, rows, cols, cin = fields.shape
    chan = mix_weight.shape[1]
    lats, lons = lax.axis_size("lat"), lax.axis_size("lon")
    x = jnp.transpose(fields, (0, 1, 3, 2))
    groups = rows * SLOT // 128
    edge = (batch, groups, cin, 128)
    west, east = pl.pallas_call(
        pack_columns,
        grid=(batch,),
        in_specs=[per_sample(x.shape)],
        out_specs=[per_sample(edge)] * 2,
        out_shape=[jax.ShapeDtypeStruct(edge, BF)] * 2,
        compiler_params=params(60),
        cost_estimate=cost(0, 4 * MIB),
        name="pack_columns",
    )(x)
    right = lax.ppermute(west, "lon", [((i + 1) % lons, i) for i in range(lons)])
    left = lax.ppermute(east, "lon", [((i - 1) % lons, i) for i in range(lons)])
    weights = (lift_weight, near_kernel, far_kernel, mix_weight)
    shapes = [(4, 256, 256), (6 * 256, 256), (256, 256)]
    strip = (batch, HALO, cin, 128)
    last = rows // 8 - 1
    p_send, q_send = pl.pallas_call(
        pack_rows,
        grid=(1,),
        in_specs=[
            pl.BlockSpec((batch, 8, cin, cols), lambda i: (0, 0, 0, 0)),
            pl.BlockSpec((batch, 8, cin, cols), lambda i: (0, last, 0, 0)),
            whole(edge),
            whole(edge),
        ],
        out_specs=[whole(strip)] * 2,
        out_shape=[jax.ShapeDtypeStruct(strip, BF)] * 2,
        compiler_params=params(60),
        cost_estimate=cost(0, 2 * MIB),
        name="pack_rows",
    )(x, x, right, left)
    p_got = lax.ppermute(p_send, ("lon", "lat"), swaps(lats, lons, 1))
    q_got = lax.ppermute(q_send, ("lon", "lat"), swaps(lats, lons, 0))

    blocks = (rows - 8) // 8
    inner = rows - 16
    fx = (batch, 2, 2, 4, 128, chan)
    made = [pltpu.VMEM(shape, BF) for shape in shapes]
    out, edges = pl.pallas_call(
        inner_rows,
        grid=(batch,),
        in_specs=[per_sample(x.shape), per_sample(edge), per_sample(edge)]
        + [whole(w.shape) for w in weights],
        out_specs=[
            pl.BlockSpec(
                (pl.Element(1), pl.Element(inner), pl.Element(cols), pl.Element(chan)),
                lambda b: (b, 8, 0, 0),
            ),
            per_sample(fx),
        ],
        out_shape=[
            jax.ShapeDtypeStruct((batch, rows, cols, chan), BF),
            jax.ShapeDtypeStruct(fx, BF),
        ],
        scratch_shapes=[
            pltpu.VMEM((8 * blocks + 2, 128, 256), BF),
            pltpu.VMEM((3, blocks, 2, 4, cols, chan), BF),
            pltpu.VMEM(((blocks - 1) * 4 * cols, 256), BF),
        ]
        + made,
        compiler_params=params(INNER_MIB),
        cost_estimate=cost(11 * 10**9, 12 * MIB),
        name="inner_rows",
    )(x, right, left, *weights)
    units = 2 * batch
    edge_rows = pl.BlockSpec((batch, 8, cin, cols), lambda i: (0, 0, 0, 0))
    last_rows = pl.BlockSpec((batch, 8, cin, cols), lambda i: (0, last, 0, 0))
    return pl.pallas_call(
        outer_rows,
        grid=(1,),
        in_specs=[edge_rows, last_rows, whole(edge), whole(edge), whole(strip), whole(strip)]
        + [whole(fx)]
        + [whole(w.shape) for w in weights]
        + [pl.BlockSpec(memory_space=pl.ANY)],
        out_specs=pl.BlockSpec(memory_space=pl.ANY),
        out_shape=jax.ShapeDtypeStruct((batch, rows, cols, chan), BF),
        scratch_shapes=[
            pltpu.VMEM((units, 12, 128, 256), BF),
            pltpu.VMEM((3, units, 2, 2, 4, cols, chan), BF),
            pltpu.VMEM((units * 4 * cols, 256), BF),
            pltpu.VMEM((units, 8, cols, chan), BF),
        ]
        + made
        + [pltpu.SemaphoreType.DMA((units,))],
        input_output_aliases={11: 0},
        compiler_params=params(OUTER_MIB),
        cost_estimate=cost(5 * 10**9, 6 * MIB),
        name="outer_rows",
    )(x, x, right, left, p_got, q_got, edges, *weights, out)


def solution(mesh):
    return jax.shard_map(
        on_device,
        mesh=mesh,
        in_specs=(P(None, "lat", "lon", None), P(), P(), P(), P()),
        out_specs=P(None, "lat", "lon", None),
        check_vma=False,
    )
```

time: 208 us -> 61.2 us (0.29)
  matrix products: 152 us -> 0 us
  Pallas kernels: 0 us -> 45.1 us
  other arithmetic: 19 us -> 0 us
  starting transfers between devices: 18 us -> 6.49 us
  waiting for transfers between devices: 16.9 us -> 7.58 us
    dot_general x19 -> x0, matrix products: 152 us -> none  [the longest x17 116 us: convolve(): jnp.einsum('bhwc,cd->bhwd', piece, kernel[row_tap, col_tap], preferred_el...]
    pallas_call x0 -> x4, Pallas kernels: none -> 45.1 us  [the longest x1 24.3 us: on_device(): pl.pallas_call(inner_rows, grid=(batch,), in_specs=[per_sample(x.shape),...]
    concatenate x5 -> x0, other arithmetic: 17.6 us -> none  [the longest x2 17.3 us: padded_2(): block = jnp.concatenate([low, block, high], axis=dim)]
    ppermute x10 -> x4, starting transfers between devices: 18 us -> 6.49 us  [the longest x1 3.33 us: on_device(): lax.ppermute(west, 'lon', [((i + 1) % lons, i) for i in range(lons)])]
    ppermute x10 -> x4, waiting for transfers between devices: 16.9 us -> 7.58 us  [the longest x1 5.69 us: on_device(): lax.ppermute(west, 'lon', [((i + 1) % lons, i) for i in range(lons)])]
  transfers between devices with their start and end apart: 10 -> 4, of which waited for: 4 -> 2; matrix products, arithmetic and copies ran while one was open for 10% -> 0% of each run, Pallas kernels for 0% -> 40%
where the time goes in v1:
time: 61.2 us; the launch traced here: 61 us
  Pallas kernels  45.1 us (74%)
  waiting for transfers between devices  7.58 us (12%)
  starting transfers between devices  6.49 us (11%)
  local copies, waits for them, and re-layouts  1.57 us (3%)
    pallas_call x1, Pallas kernels, on_device(): pl.pallas_call(inner_rows, grid=(batch,), in_specs=[per_sample(x.shape),...  24.3 us
    pallas_call x1, Pallas kernels, on_device(): pl.pallas_call(outer_rows, grid=(1,), in_specs=[edge_rows, last_rows, who...  13.2 us
    ppermute x1, waiting for transfers between devices, on_device(): lax.ppermute(west, 'lon', [((i + 1) % lons, i) for i in range(lons)])  5.69 us
    pallas_call x1, Pallas kernels, on_device(): pl.pallas_call(pack_columns, grid=(batch,), in_specs=[per_sample(x.shape)...  4.82 us
    ppermute x1, starting transfers between devices, on_device(): lax.ppermute(west, 'lon', [((i + 1) % lons, i) for i in range(lons)])  3.33 us
    pallas_call x1, Pallas kernels, on_device(): pl.pallas_call(pack_rows, grid=(1,), in_specs=[pl.BlockSpec((batch, 8, ci...  2.76 us
    ppermute x1, starting transfers between devices, on_device(): q_got = lax.ppermute(q_send, ('lon', 'lat'), swaps(lats, lons, 0))  2.65 us
    ppermute x1, waiting for transfers between devices, on_device(): left = lax.ppermute(east, 'lon', [((i - 1) % lons, i) for i in range(lons)])  1.88 us
  transfers between devices with their start and end apart: 4, of which 2 were waited for; matrix products, arithmetic and copies ran while one was open for 0% of the time, Pallas kernels for 40%

profile of v1, /device:TPU:0, one launch (start us, length us, event | category | flops | bytes accessed | tf_op | source)
XLA Modules:
  0.0 61.0 jit_solution(11273508144898199349)
XLA Ops:
  0.0 4.8 %pack_columns.1 = (bf16[4,3,80,128]{3,2,1,0:T(8,128)(2,1)}, bf16[4,3,80,128]{3,2,1,0:T(8,128)(2,1)}) custom-call(bf16[4,48,80,112]{3,2,1,0:T(8,128)(2,1)} %bitcast.1), custom_call_target="tpu_custom_call" | custom-call | bytes 4194304 | tf_op jit(solution)/shard_map/pack_columns/pallas_call | solution.py:267
  4.8 3.3 %collective-permute-start = (bf16[4,3,80,128]{3,2,1,0:T(8,128)(2,1)}, bf16[4,3,80,128]{3,2,1,0:T(8,128)(2,1)S(1)}, u32[]{:S(2)}, u32[]{:S(2)}) collective-permute-start(bf16[4,3,80,128]{3,2,1,0:T(8,128)(2,1)} %get-tuple-element.11), channel_id=1, source_target_pairs={{4,0},{8,4},{12,8},{16,12},{20,16},{24,20},{28,24},{0,28},{5,1},{9... | collective-permute-start | bytes 737288 | tf_op jit(solution)/shard_map/ppermute | solution.py:277
  8.2 0.0 collective-permute-start.1
  8.2 5.7 %collective-permute-done.right_ref = bf16[4,3,80,128]{3,2,1,0:T(8,128)(2,1)S(1)} collective-permute-done((bf16[4,3,80,128]{3,2,1,0:T(8,128)(2,1)}, bf16[4,3,80,128]{3,2,1,0:T(8,128)(2,1)S(1)}, u32[]{:S(2)}, u32[]{:S(2)}) %collective-permute-start) | collective-permute-done | bytes 245792 | tf_op jit(solution)/shard_map/ppermute | solution.py:277
  13.9 0.0 copy-start
  13.9 1.9 %collective-permute-done.1.left_ref = bf16[4,3,80,128]{3,2,1,0:T(8,128)(2,1)S(1)} collective-permute-done((bf16[4,3,80,128]{3,2,1,0:T(8,128)(2,1)}, bf16[4,3,80,128]{3,2,1,0:T(8,128)(2,1)S(1)}, u32[]{:S(2)}, u32[]{:S(2)}) %collective-permute-start.1) | collective-permute-done | bytes 245792 | tf_op jit(solution)/shard_map/ppermute | solution.py:278
  15.7 0.0 copy-done
  15.7 0.0 copy-start.1
  15.7 0.7 %copy-done.1 = bf16[4,3,80,128]{3,2,1,0:T(8,128)(2,1)} copy-done((bf16[4,3,80,128]{3,2,1,0:T(8,128)(2,1)}, bf16[4,3,80,128]{3,2,1,0:T(8,128)(2,1)S(1)}, u32[]{:S(2)}) %copy-start.1) | copy-done | bytes 245784
  16.4 2.8 %pack_rows.1 = (bf16[4,5,80,128]{3,2,1,0:T(8,128)(2,1)}, bf16[4,5,80,128]{3,2,1,0:T(8,128)(2,1)}) custom-call(bf16[4,48,80,112]{3,2,1,0:T(8,128)(2,1)} %bitcast.2, bf16[4,48,80,112]{3,2,1,0:T(8,128)(2,1)} %bitcast.3, bf16[4,3,80,128]{3,2,1,0:T(8,128)(2,1)} %copy-done, bf16[4,3,80,128]{3,2,1,0:T(8,128)(2,1)} %copy-done.1), custom_call_target="tpu_custom_call" | custom-call | bytes 2097152 | tf_op jit(solution)/shard_map/pack_rows/pallas_call | solution.py:283
  19.2 0.5 collective-permute-start.2
  19.7 2.6 %collective-permute-start.3 = (bf16[4,5,80,128]{3,2,1,0:T(8,128)(2,1)}, bf16[4,5,80,128]{3,2,1,0:T(8,128)(2,1)S(1)}, u32[]{:S(2)}, u32[]{:S(2)}) collective-permute-start(bf16[4,5,80,128]{3,2,1,0:T(8,128)(2,1)} %get-tuple-element.14), channel_id=1, source_target_pairs={{1,0},{5,4},{9,8},{13,12},{17,16},{21,20},{25,24},{29,28},{0,1},{4... | collective-permute-start | bytes 1228808 | tf_op jit(solution)/shard_map/ppermute | solution.py:299
  22.3 24.3 %inner_rows.1 = (bf16[4,48,112,128]{3,2,1,0:T(8,128)(2,1)}, bf16[4,2,2,4,128,128]{5,4,3,2,1,0:T(8,128)(2,1)}) custom-call(bf16[4,48,80,112]{3,2,1,0:T(8,128)(2,1)} %bitcast.4, bf16[4,3,80,128]{3,2,1,0:T(8,128)(2,1)} %copy-done, bf16[4,3,80,128]{3,2,1,0:T(8,128)(2,1)} %copy-done.1, bf16[80,128]{1,0:T(8,128)(2,1)} %lift_ref.3, ...), custom_call_target="tpu_custom_call" | custom-call | flops 11000000512 | bytes 12582912 | tf_op jit(solution)/shard_map/inner_rows/pallas_call | solution.py:305
  46.7 0.0 collective-permute-done.2.p_ref
  46.7 0.0 copy-start.2
  46.7 0.0 collective-permute-done.3.q_ref
  46.7 0.0 copy-start.3
  46.7 0.7 %copy-done.2 = bf16[4,5,80,128]{3,2,1,0:T(8,128)(2,1)} copy-done((bf16[4,5,80,128]{3,2,1,0:T(8,128)(2,1)}, bf16[4,5,80,128]{3,2,1,0:T(8,128)(2,1)S(1)}, u32[]{:S(2)}) %copy-start.2) | copy-done | bytes 409624
  47.4 0.1 copy-done.3
  47.6 13.2 %outer_rows.1 = bf16[4,48,112,128]{3,2,1,0:T(8,128)(2,1)} custom-call(bf16[4,48,80,112]{3,2,1,0:T(8,128)(2,1)} %bitcast.5, bf16[4,48,80,112]{3,2,1,0:T(8,128)(2,1)} %bitcast.6, bf16[4,3,80,128]{3,2,1,0:T(8,128)(2,1)} %copy-done, bf16[4,3,80,128]{3,2,1,0:T(8,128)(2,1)} %copy-done.1, ...), custom_call_target="tpu_custom_call", output_to_operand_aliasing={{}: (11, {})} | custom-call | flops 5000000000 | bytes 6291456 | tf_op jit(solution)/shard_map/outer_rows/pallas_call | solution.py:334
Async XLA Ops:
  4.8 9.0 %collective-permute-start = (bf16[4,3,80,128]{3,2,1,0:T(8,128)(2,1)}, bf16[4,3,80,128]{3,2,1,0:T(8,128)(2,1)S(1)}, u32[]{:S(2)}, u32[]{:S(2)}) collective-permute-start(bf16[4,3,80,128]{3,2,1,0:T(8,128)(2,1)} %get-tuple-element.11), channel_id=1, source_target_pairs={{4,0},{8,4},{12,8},{16,12},{20,16},{24,20},{28,24},{0,28},{5,1},{9... | collective-permute-start | bytes 737288 | tf_op jit(solution)/shard_map/ppermute | solution.py:277
  8.2 7.6 %collective-permute-start.1 = (bf16[4,3,80,128]{3,2,1,0:T(8,128)(2,1)}, bf16[4,3,80,128]{3,2,1,0:T(8,128)(2,1)S(1)}, u32[]{:S(2)}, u32[]{:S(2)}) collective-permute-start(bf16[4,3,80,128]{3,2,1,0:T(8,128)(2,1)} %get-tuple-element.12), channel_id=1, source_target_pairs={{28,0},{0,4},{4,8},{8,12},{12,16},{16,20},{20,24},{24,28},{29,1},{... | collective-permute-start | bytes 737288 | tf_op jit(solution)/shard_map/ppermute | solution.py:278
  13.9 1.9 %copy-start = (bf16[4,3,80,128]{3,2,1,0:T(8,128)(2,1)}, bf16[4,3,80,128]{3,2,1,0:T(8,128)(2,1)S(1)}, u32[]{:S(2)}) copy-start(bf16[4,3,80,128]{3,2,1,0:T(8,128)(2,1)S(1)} %collective-permute-done.right_ref) | copy-start | bytes 737284
  15.7 0.7 %copy-start.1 = (bf16[4,3,80,128]{3,2,1,0:T(8,128)(2,1)}, bf16[4,3,80,128]{3,2,1,0:T(8,128)(2,1)S(1)}, u32[]{:S(2)}) copy-start(bf16[4,3,80,128]{3,2,1,0:T(8,128)(2,1)S(1)} %collective-permute-done.1.left_ref) | copy-start | bytes 737284
  19.2 27.5 %collective-permute-start.2 = (bf16[4,5,80,128]{3,2,1,0:T(8,128)(2,1)}, bf16[4,5,80,128]{3,2,1,0:T(8,128)(2,1)S(1)}, u32[]{:S(2)}, u32[]{:S(2)}) collective-permute-start(bf16[4,5,80,128]{3,2,1,0:T(8,128)(2,1)} %get-tuple-element.13), channel_id=1, source_target_pairs={{16,0},{20,4},{24,8},{28,12},{0,16},{4,20},{8,24},{12,28},{2,1},{6... | collective-permute-start | bytes 1228808 | tf_op jit(solution)/shard_map/ppermute | solution.py:298
  19.7 27.0 %collective-permute-start.3 = (bf16[4,5,80,128]{3,2,1,0:T(8,128)(2,1)}, bf16[4,5,80,128]{3,2,1,0:T(8,128)(2,1)S(1)}, u32[]{:S(2)}, u32[]{:S(2)}) collective-permute-start(bf16[4,5,80,128]{3,2,1,0:T(8,128)(2,1)} %get-tuple-element.14), channel_id=1, source_target_pairs={{1,0},{5,4},{9,8},{13,12},{17,16},{21,20},{25,24},{29,28},{0,1},{4... | collective-permute-start | bytes 1228808 | tf_op jit(solution)/shard_map/ppermute | solution.py:299
  46.7 0.8 %copy-start.2 = (bf16[4,5,80,128]{3,2,1,0:T(8,128)(2,1)}, bf16[4,5,80,128]{3,2,1,0:T(8,128)(2,1)S(1)}, u32[]{:S(2)}) copy-start(bf16[4,5,80,128]{3,2,1,0:T(8,128)(2,1)S(1)} %collective-permute-done.2.p_ref) | copy-start | bytes 1228804
  46.7 0.9 %copy-start.3 = (bf16[4,5,80,128]{3,2,1,0:T(8,128)(2,1)}, bf16[4,5,80,128]{3,2,1,0:T(8,128)(2,1)S(1)}, u32[]{:S(2)}) copy-start(bf16[4,5,80,128]{3,2,1,0:T(8,128)(2,1)S(1)} %collective-permute-done.3.q_ref) | copy-start | bytes 1228804

commit v2 on v1

v2 whole, which is shorter than its diff:
```python
import functools

import jax
import jax.numpy as jnp
from jax import lax
from jax.experimental import pallas as pl
from jax.experimental.pallas import tpu as pltpu
from jax.sharding import PartitionSpec as P

FAR = 4
BF = jnp.bfloat16
F32 = jnp.float32
HALO = 5
SLOT = 8
MIB = 1 << 20
FIRST_MIB = 16
INNER_MIB = 24
OUTER_MIB = 34
PACK_MIB = 12


def dot(a, b):
    return jnp.dot(a, b, preferred_element_type=F32)


def silu_of_half(h):
    return h + h * jnp.tanh(h)


def turned(v, shift):
    shift %= 128
    if shift == 0:
        return v
    return jnp.concatenate([v[:, 128 - shift :], v[:, : 128 - shift]], axis=1)


def widened(row):
    return jnp.concatenate([row, jnp.zeros((row.shape[0], 128 - row.shape[1]), BF)], axis=1)


def with_columns(row, right_ref, left_ref, lead, r):
    per = 128 // SLOT
    cols = row.shape[1]
    at = (r % per) * SLOT
    right = turned(right_ref[lead, r // per], cols - at)
    left = turned(left_ref[lead, r // per], 128 - SLOT - at)
    return jnp.concatenate([row, right[:, cols : cols + SLOT], left[:, cols + SLOT :]], axis=1)


def three_taps(row):
    before = jnp.concatenate([row[:, 127:], row[:, :127]], axis=1)
    after = jnp.concatenate([row[:, 1:], row[:, :1]], axis=1)
    fill = jnp.zeros((256 - 3 * row.shape[0], 128), BF)
    return jnp.concatenate([before, row, after, fill], axis=0).T


def pack_columns(*refs):
    *x_refs, west_ref, east_ref = refs
    lane = lax.broadcasted_iota(jnp.int32, (west_ref.shape[2], 128), 1)
    for group, x_ref in enumerate(x_refs):
        cols = x_ref.shape[3]
        rows = [widened(x_ref[0, i]) for i in range(x_ref.shape[1])]
        for start, ref in ((0, west_ref), (cols - SLOT, east_ref)):
            moved = [turned(row, i * SLOT - start) for i, row in enumerate(rows)]
            packed = moved[0]
            for i, row in enumerate(moved):
                packed = jnp.where(lane < i * SLOT, packed, row)
            ref[0, group] = packed


def make_near(lift_ref, near_ref, wn_ref):
    cin, chan = lift_ref.shape
    wn_ref[...] = jnp.zeros_like(wn_ref)
    for a in range(3):
        for b in range(3):
            near = (0.5 * dot(lift_ref[...], near_ref[a, b])).astype(BF)
            for o in range(2):
                wn_ref[a + o, b * cin : (b + 1) * cin, o * chan : (o + 1) * chan] = near


def make_far(far_ref, mix_ref, wf_ref, wm_ref):
    chan = mix_ref.shape[0]
    wf_ref[...] = jnp.zeros_like(wf_ref)
    wm_ref[...] = jnp.zeros_like(wm_ref)
    for a in range(3):
        for b in range(3):
            far = (0.5 * far_ref[a, b].astype(F32)).astype(BF)
            for o in range(2):
                k = a + o
                base = (2 * b + k // 2) * 256 + (k % 2) * chan
                wf_ref[base : base + chan, o * chan : (o + 1) * chan] = far
    wm_ref[:chan, :chan] = mix_ref[...]
    wm_ref[chan:, chan:] = mix_ref[...]


def pack_rows(rows, top_ref, bottom_ref, right_ref, left_ref, p_ref, q_ref):
    even = lax.rem(lax.axis_index("lat"), 2) == 0
    top, bottom = [], []
    for k in range(HALO):
        top.append(with_columns(top_ref[0, k], right_ref, left_ref, 0, k))
        r = rows - HALO + k
        bottom.append(with_columns(bottom_ref[0, 8 - HALO + k], right_ref, left_ref, 0, r))
    for k in range(HALO):
        p_ref[0, k] = jnp.where(even, top[k], bottom[k])
        q_ref[0, k] = jnp.where(even, bottom[k], top[k])


def spread(f2, at, piece):
    inner = f2.shape[-2]
    f2[(0, *at)] = jnp.concatenate([piece[128 - FAR :], piece[: inner - FAR]], axis=0)
    f2[(1, *at)] = piece[:inner]
    f2[(2, *at)] = piece[FAR : inner + FAR]


def near_block(rows, wn_ref):
    lhs = jnp.concatenate(
        [jnp.concatenate([pair[i] for pair in rows], axis=0) for i in range(4)], axis=1
    )
    return silu_of_half(dot(lhs, wn_ref[...].reshape(4 * 256, 256)))


def far_block(f2, lead, g, wf_ref):
    lhs = jnp.concatenate(
        [
            jnp.concatenate([f2[(b, *lead, g + k, h, c)] for c in range(4)], axis=0)
            for b in range(3)
            for k in range(2)
            for h in range(2)
        ],
        axis=1,
    )
    return silu_of_half(dot(lhs, wf_ref[...])).astype(BF)


def halves(v, pair, height):
    base = height * pair
    return [v[base : base + height, 128 * o : 128 * o + 128] for o in range(2)]


def first_rows(x_ref, lift_ref, near_ref, first_ref, x3, wn_ref):
    @pl.when(pl.program_id(0) == 0)
    def _():
        make_near(lift_ref, near_ref, wn_ref)

    cols = x_ref.shape[3]
    for i in range(x3.shape[0]):
        x3[i] = three_taps(widened(x_ref[0, i + FAR - 1]))[:cols]
    for m in range(first_ref.shape[1]):
        rows = [[x3[8 * m + 2 * p + i] for i in range(4)] for p in range(4)]
        v = near_block(rows, wn_ref).astype(BF)
        for p in range(4):
            for o, piece in enumerate(halves(v, p, cols)):
                h, c = divmod(2 * p + o, 4)
                first_ref[0, m, h, c] = piece


def joined(main, strip):
    end = main.shape[0]
    head = jnp.concatenate([strip[14:15], main[:16].astype(F32)[1:]], axis=0)
    tail = jnp.concatenate([main[end - 16 :].astype(F32)[:15], strip[1:2]], axis=0)
    beyond = jnp.concatenate([strip[2:6], strip[2:10], strip[10:14]], axis=0)
    return jnp.concatenate(
        [head.astype(BF), main[16 : end - 16], tail.astype(BF), beyond.astype(BF)], axis=0
    )


def inner_rows(
    first_ref, west_ref, east_ref, right_ref, left_ref, lift_ref, near_ref, far_ref, mix_ref,
    out_ref, fx_ref, strips, f2, s, wn_ref, wf_ref, wm_ref,
):
    @pl.when(pl.program_id(0) == 0)
    def _():
        make_near(lift_ref, near_ref, wn_ref)
        make_far(far_ref, mix_ref, wf_ref, wm_ref)

    blocks = f2.shape[1]
    cols = f2.shape[-2]
    per = 128 // SLOT
    lane = lax.rem(lax.broadcasted_iota(jnp.int32, (lift_ref.shape[0], 128), 1), SLOT)
    for g in range(west_ref.shape[1]):
        right = jnp.where(lane < 2, turned(east_ref[0, g], -6), turned(right_ref[0, g], 2))
        left = jnp.where(lane < 6, turned(left_ref[0, g], -2), turned(west_ref[0, g], 6))
        right, left = three_taps(right), three_taps(left)
        for i in range(per):
            at = slice(SLOT * i, SLOT * i + SLOT)
            strips[per * g + i] = jnp.concatenate([right[at], left[at]], axis=0)
    low = FAR - 1
    pairs = 4 * blocks
    rows = [[strips[low + 2 * q + i] for i in range(4)] for q in range(pairs)]
    v = near_block(rows, wn_ref)
    for q in range(pairs):
        m, p = divmod(q, 4)
        for o, strip in enumerate(halves(v, q, 16)):
            h, c = divmod(2 * p + o, 4)
            piece = joined(first_ref[0, m, h, c], strip)
            spread(f2, (m, h, c), piece)
            if m == 0:
                fx_ref[0, 0, h, c] = piece
            if m == blocks - 1:
                fx_ref[0, 1, h, c] = piece
    span = 4 * cols
    for g in range(blocks - 1):
        s[g * span : (g + 1) * span] = far_block(f2, (), g, wf_ref)
    y = dot(s[...], wm_ref[...]).astype(BF)
    for g in range(blocks - 1):
        for c in range(4):
            at = g * span + c * cols
            for h in range(2):
                out_ref[0, 8 * g + 4 * h + c] = y[at : at + cols, 128 * h : 128 * h + 128]


def outer_rows(
    top_ref, bottom_ref, right_ref, left_ref, p_ref, q_ref, fx_ref,
    lift_ref, near_ref, far_ref, mix_ref, _, out_ref,
    x3, f2, s, y, wn_ref, wf_ref, wm_ref, sems,
):
    make_near(lift_ref, near_ref, wn_ref)
    make_far(far_ref, mix_ref, wf_ref, wm_ref)
    lat = lax.axis_index("lat")
    even = lax.rem(lat, 2) == 0
    poles = (lat == 0, lat == lax.axis_size("lat") - 1)
    cols = f2.shape[-2]
    total = out_ref.shape[1]
    span = 4 * cols
    units = [(b, side) for b in range(top_ref.shape[0]) for side in range(2)]
    for u, (b, side) in enumerate(units):
        pole = poles[side]
        moved = pole if side == 0 else jnp.logical_not(pole)
        from_p = even if side == 0 else jnp.logical_not(even)
        base = jnp.where(moved, 1, 0)
        close = jnp.where(moved, 0, HALO - 1)
        for k in range(HALO):
            taps = three_taps(jnp.where(from_p, p_ref[b, k], q_ref[b, k]))
            x3[u, base + k] = taps
        x3[u, 6 if side == 0 else 11] = x3[u, base + close]
        own = top_ref if side == 0 else bottom_ref
        for k in range(HALO):
            r = k if side == 0 else total - HALO + k
            t = k if side == 0 else 8 - HALO + k
            taps = three_taps(with_columns(own[b, t], right_ref, left_ref, b, r))
            x3[u, (7 if side == 0 else 6) + k] = taps
            if k == (0 if side == 0 else HALO - 1):
                x3[u, jnp.where(moved, 0, HALO)] = taps
    for u, (b, side) in enumerate(units):
        pole = poles[side]
        v = near_block(
            [[x3[u, first + i] for i in range(4)] for first in (0, 2, 6, 8)], wn_ref
        ).astype(BF)
        for q in range(2):
            for o, piece in enumerate(halves(v, q, 128)):
                c = 2 * q + o
                spread(f2, (u, side, side, jnp.where(pole, 3 - c, c)), piece)
            for o, piece in enumerate(halves(v, 2 + q, 128)):
                spread(f2, (u, side, 1 - side, 2 * q + o), piece)
        for h in range(2):
            for c in range(4):
                spread(f2, (u, 1 - side, h, c), fx_ref[b, side, h, c])
    for u in range(len(units)):
        s[u * span : (u + 1) * span] = far_block(f2, (u,), 0, wf_ref)
    copies = []
    for u, (b, side) in enumerate(units):
        done = dot(s[u * span : (u + 1) * span], wm_ref[...]).astype(BF)
        for c in range(4):
            for h in range(2):
                y[u, 4 * h + c] = done[cols * c : cols * c + cols, 128 * h : 128 * h + 128]
        to = out_ref.at[b, pl.ds(0 if side == 0 else total - 8, 8)]
        copy = pltpu.make_async_copy(y.at[u], to, sems.at[u])
        copy.start()
        copies.append(copy)
    for copy in copies:
        copy.wait()


def whole(shape):
    return pl.BlockSpec(shape, lambda *_: (0,) * len(shape))


def per_sample(shape):
    return pl.BlockSpec((1,) + shape[1:], lambda b, *_: (b,) + (0,) * (len(shape) - 1))


def params(mib):
    return pltpu.CompilerParams(vmem_limit_bytes=mib * MIB)


def cost(flops, nbytes):
    return pl.CostEstimate(flops=flops, bytes_accessed=nbytes, transcendentals=0)


def swaps(lats, lons, offset):
    half = lons // 2
    pairs = []
    for lat in range(lats):
        other = lat + (1 if (lat + offset) % 2 == 0 else -1)
        for lon in range(lons):
            if 0 <= other < lats:
                pairs.append((lon * lats + other, lon * lats + lat))
            else:
                pairs.append(((lon + half) % lons * lats + lat, lon * lats + lat))
    return pairs


def made_weights():
    return [pltpu.VMEM(shape, BF) for shape in ((4, 256, 256), (6 * 256, 256), (256, 256))]


def edge_shape(x):
    per = 128 // SLOT
    return (x.shape[0], -(-x.shape[1] // per), x.shape[2], 128)


def call_pack(x):
    edge = edge_shape(x)
    return pl.pallas_call(
        pack_columns,
        grid=(x.shape[0],),
        in_specs=[
            pl.BlockSpec(
                (1, 128 // SLOT, x.shape[2], x.shape[3]), functools.partial(lambda g, b: (b, g, 0, 0), g)
            )
            for g in range(edge[1])
        ],
        out_specs=[per_sample(edge)] * 2,
        out_shape=[jax.ShapeDtypeStruct(edge, BF)] * 2,
        compiler_params=params(PACK_MIB),
        cost_estimate=cost(0, 4 * MIB),
        name="pack_columns",
    )(*[x] * edge[1])


def call_first(x, weights):
    batch, rows, _, cols = x.shape
    chan = weights[-1].shape[1]
    first = (batch, rows // 8 - 1, 2, 4, cols, chan)
    return pl.pallas_call(
        first_rows,
        grid=(batch,),
        in_specs=[per_sample(x.shape)] + [whole(w.shape) for w in weights[:2]],
        out_specs=per_sample(first),
        out_shape=jax.ShapeDtypeStruct(first, BF),
        scratch_shapes=[pltpu.VMEM((rows - 6, cols, 256), BF), made_weights()[0]],
        compiler_params=params(FIRST_MIB),
        cost_estimate=cost(6 * 10**9, 9 * MIB),
        name="first_rows",
    )(x, *weights[:2])


def call_inner(first, west, east, right, left, weights, rows):
    batch, blocks, _, _, cols, chan = first.shape
    fx = (batch, 2, 2, 4, 128, chan)
    inner = rows - 16
    return pl.pallas_call(
        inner_rows,
        grid=(batch,),
        in_specs=[per_sample(first.shape)]
        + [per_sample(right.shape)] * 4
        + [whole(w.shape) for w in weights],
        out_specs=[
            pl.BlockSpec(
                (pl.Element(1), pl.Element(inner), pl.Element(cols), pl.Element(chan)),
                lambda b: (b, 8, 0, 0),
            ),
            per_sample(fx),
        ],
        out_shape=[
            jax.ShapeDtypeStruct((batch, rows, cols, chan), BF),
            jax.ShapeDtypeStruct(fx, BF),
        ],
        scratch_shapes=[
            pltpu.VMEM((rows, 16, 256), BF),
            pltpu.VMEM((3, blocks, 2, 4, cols, chan), BF),
            pltpu.VMEM(((blocks - 1) * 4 * cols, 256), BF),
        ]
        + made_weights(),
        compiler_params=params(INNER_MIB),
        cost_estimate=cost(7 * 10**9, 12 * MIB),
        name="inner_rows",
    )(first, west, east, right, left, *weights)


def on_device(fields, lift_weight, near_kernel, far_kernel, mix_weight):
    batch, rows, cols, cin = fields.shape
    chan = mix_weight.shape[1]
    lats, lons = lax.axis_size("lat"), lax.axis_size("lon")
    x = jnp.transpose(fields, (0, 1, 3, 2))
    edge = edge_shape(x)
    west, east = call_pack(x)
    right = lax.ppermute(west, "lon", [((i + 1) % lons, i) for i in range(lons)])
    left = lax.ppermute(east, "lon", [((i - 1) % lons, i) for i in range(lons)])
    weights = (lift_weight, near_kernel, far_kernel, mix_weight)
    first = call_first(x, weights)
    strip = (batch, HALO, cin, 128)
    last = rows // 8 - 1
    p_send, q_send = pl.pallas_call(
        functools.partial(pack_rows, rows),
        grid=(batch,),
        in_specs=[
            pl.BlockSpec((1, 8, cin, cols), lambda b: (b, 0, 0, 0)),
            pl.BlockSpec((1, 8, cin, cols), lambda b: (b, last, 0, 0)),
            per_sample(edge),
            per_sample(edge),
        ],
        out_specs=[per_sample(strip)] * 2,
        out_shape=[jax.ShapeDtypeStruct(strip, BF)] * 2,
        compiler_params=params(PACK_MIB),
        cost_estimate=cost(0, 2 * MIB),
        name="pack_rows",
    )(x, x, right, left)
    p_got = lax.ppermute(p_send, ("lon", "lat"), swaps(lats, lons, 1))
    q_got = lax.ppermute(q_send, ("lon", "lat"), swaps(lats, lons, 0))

    out, edges = call_inner(first, west, east, right, left, weights, rows)
    units = 2 * batch
    fx = edges.shape
    made = made_weights()
    edge_rows = pl.BlockSpec((batch, 8, cin, cols), lambda i: (0, 0, 0, 0))
    last_rows = pl.BlockSpec((batch, 8, cin, cols), lambda i: (0, last, 0, 0))
    return pl.pallas_call(
        outer_rows,
        grid=(1,),
        in_specs=[edge_rows, last_rows, whole(edge), whole(edge), whole(strip), whole(strip)]
        + [whole(fx)]
        + [whole(w.shape) for w in weights]
        + [pl.BlockSpec(memory_space=pl.ANY)],
        out_specs=pl.BlockSpec(memory_space=pl.ANY),
        out_shape=jax.ShapeDtypeStruct((batch, rows, cols, chan), BF),
        scratch_shapes=[
            pltpu.VMEM((units, 12, 128, 256), BF),
            pltpu.VMEM((3, units, 2, 2, 4, cols, chan), BF),
            pltpu.VMEM((units * 4 * cols, 256), BF),
            pltpu.VMEM((units, 8, cols, chan), BF),
        ]
        + made
        + [pltpu.SemaphoreType.DMA((units,))],
        input_output_aliases={11: 0},
        compiler_params=params(OUTER_MIB),
        cost_estimate=cost(5 * 10**9, 6 * MIB),
        name="outer_rows",
    )(x, x, right, left, p_got, q_got, edges, *weights, out)


def solution(mesh):
    return jax.shard_map(
        on_device,
        mesh=mesh,
        in_specs=(P(None, "lat", "lon", None), P(), P(), P(), P()),
        out_specs=P(None, "lat", "lon", None),
        check_vma=False,
    )
```

time: 61.2 us -> 45.9 us (0.75)
  Pallas kernels: 45.1 us -> 36.7 us
  waiting for transfers between devices: 7.58 us -> 0.01 us
    pallas_call x3 -> x4, Pallas kernels: 31.9 us -> 25.8 us  [the longest x1 13 us: call_inner(): pl.pallas_call(inner_rows, grid=(batch,), in_specs=[per_sample(first.shap...]
    ppermute x1, waiting for transfers between devices: 5.69 us -> 0.01 us  [on_device(): lax.ppermute(west, 'lon', [((i + 1) % lons, i) for i in range(lons)])]
    pallas_call x1, Pallas kernels: 13.2 us -> 10.9 us  [on_device(): pl.pallas_call(outer_rows, grid=(1,), in_specs=[edge_rows, last_rows, who...]
    ppermute x1, waiting for transfers between devices: 1.88 us -> 0.01 us  [on_device(): left = lax.ppermute(east, 'lon', [((i - 1) % lons, i) for i in range(lons)])]
    unnamed x8 -> x12, local copies, waits for them, and re-layouts: 1.57 us -> 2.14 us
  transfers between devices with their start and end apart: 4 -> 4, of which waited for: 2 -> 0; matrix products, arithmetic and copies ran while one was open for 0% -> 0% of each run, Pallas kernels for 40% -> 50%
where the time goes in v2:
time: 45.9 us; the launch traced here: 45.7 us
  Pallas kernels  36.7 us (80%)
  starting transfers between devices  6.61 us (14%)
  local copies, waits for them, and re-layouts  2.14 us (5%)
    pallas_call x1, Pallas kernels, call_inner(): pl.pallas_call(inner_rows, grid=(batch,), in_specs=[per_sample(first.shap...  13 us
    pallas_call x1, Pallas kernels, on_device(): pl.pallas_call(outer_rows, grid=(1,), in_specs=[edge_rows, last_rows, who...  10.9 us
    pallas_call x1, Pallas kernels, call_first(): pl.pallas_call(first_rows, grid=(batch,), in_specs=[per_sample(x.shape)]...  9.87 us
    ppermute x1, starting transfers between devices, on_device(): lax.ppermute(west, 'lon', [((i + 1) % lons, i) for i in range(lons)])  3.39 us
    ppermute x1, starting transfers between devices, on_device(): q_got = lax.ppermute(q_send, ('lon', 'lat'), swaps(lats, lons, 0))  2.65 us
    pallas_call x1, Pallas kernels, call_pack(): pl.pallas_call(pack_columns, grid=(x.shape[0],), in_specs=[pl.BlockSpec((...  2.2 us
    unnamed x12, local copies, waits for them, and re-layouts  2.14 us
  transfers between devices with their start and end apart: 4, of which 0 were waited for; matrix products, arithmetic and copies ran while one was open for 0% of the time, Pallas kernels for 50%

profile of v2, /device:TPU:0, one launch (start us, length us, event | category | flops | bytes accessed | tf_op | source)
XLA Modules:
  0.0 45.7 jit_solution(6852497215491216615)
XLA Ops:
  0.0 0.0 copy-start
  0.0 2.1 %copy-done = bf16[4,48,112,80]{2,3,1,0:T(8,128)(2,1)S(1)} copy-done((bf16[4,48,112,80]{2,3,1,0:T(8,128)(2,1)S(1)}, bf16[4,48,112,80]{2,3,1,0:T(8,128)(2,1)}, u32[]{:S(2)}) %copy-start) | copy-done | bytes 3440664
  2.1 0.0 copy-start.1
  2.1 0.0 copy-start.2
  2.1 2.2 %pack_columns.1 = (bf16[4,3,80,128]{3,2,1,0:T(8,128)(2,1)S(1)}, bf16[4,3,80,128]{3,2,1,0:T(8,128)(2,1)S(1)}) custom-call(bf16[4,48,80,112]{3,2,1,0:T(8,128)(2,1)S(1)} %bitcast.1, bf16[4,48,80,112]{3,2,1,0:T(8,128)(2,1)S(1)} %bitcast.2, bf16[4,48,80,112]{3,2,1,0:T(8,128)(2,1)S(1)} %bitcast.3), custom_call_target="tpu_custom_call" | custom-call | bytes 4194304 | tf_op jit(solution)/shard_map/pack_columns/pallas_call | solution.py:314
  4.3 3.4 %collective-permute-start = (bf16[4,3,80,128]{3,2,1,0:T(8,128)(2,1)S(1)}, bf16[4,3,80,128]{3,2,1,0:T(8,128)(2,1)S(1)}, u32[]{:S(2)}, u32[]{:S(2)}) collective-permute-start(bf16[4,3,80,128]{3,2,1,0:T(8,128)(2,1)S(1)} %get-tuple-element.11.west_ref), channel_id=1, source_target_pairs={{4,0},{8,4},{12,8},{16,12},{20,16},{24,20},{28,24},{0,28},{5,1},{9... | collective-permute-start | bytes 737288 | tf_op jit(solution)/shard_map/ppermute | solution.py:388
  7.7 0.0 collective-permute-start.1
  7.7 0.0 copy-done.1
  7.7 0.0 copy-done.2
  7.7 0.0 copy-done.5
  7.7 9.9 %first_rows.1.first_ref = bf16[4,5,2,4,112,128]{5,4,3,2,1,0:T(8,128)(2,1)S(1)} custom-call(bf16[4,48,80,112]{3,2,1,0:T(8,128)(2,1)S(1)} %bitcast.4, bf16[80,128]{1,0:T(8,128)(2,1)S(1)} %copy-done.5, bf16[3,3,128,128]{3,2,1,0:T(8,128)(2,1)S(1)} %copy-done.2), custom_call_target="tpu_custom_call" | custom-call | flops 6000000000 | bytes 9437184 | tf_op jit(solution)/shard_map/first_rows/pallas_call | solution.py:335
  17.6 0.0 copy-start.3
  17.6 0.0 copy-start.4
  17.6 0.0 collective-permute-done.right_ref
  17.7 0.0 collective-permute-done.1.left_ref
  17.7 0.7 %pack_rows.1 = (bf16[4,5,80,128]{3,2,1,0:T(8,128)(2,1)S(1)}, bf16[4,5,80,128]{3,2,1,0:T(8,128)(2,1)S(1)}) custom-call(bf16[4,48,80,112]{3,2,1,0:T(8,128)(2,1)S(1)} %bitcast.5, bf16[4,48,80,112]{3,2,1,0:T(8,128)(2,1)S(1)} %bitcast.6, bf16[4,3,80,128]{3,2,1,0:T(8,128)(2,1)S(1)} %collective-permute-done.right_ref, ...), custom_call_target="tpu_custom_call" | custom-call | bytes 2097152 | tf_op jit(solution)/shard_map/pack_rows/pallas_call | solution.py:394
  18.4 0.6 %collective-permute-start.2 = (bf16[4,5,80,128]{3,2,1,0:T(8,128)(2,1)S(1)}, bf16[4,5,80,128]{3,2,1,0:T(8,128)(2,1)S(1)}, u32[]{:S(2)}, u32[]{:S(2)}) collective-permute-start(bf16[4,5,80,128]{3,2,1,0:T(8,128)(2,1)S(1)} %get-tuple-element.13), channel_id=1, source_target_pairs={{16,0},{20,4},{24,8},{28,12},{0,16},{4,20},{8,24},{12,28},{2,1},{6... | collective-permute-start | bytes 1228808 | tf_op jit(solution)/shard_map/ppermute | solution.py:409
  19.0 2.6 %collective-permute-start.3 = (bf16[4,5,80,128]{3,2,1,0:T(8,128)(2,1)S(1)}, bf16[4,5,80,128]{3,2,1,0:T(8,128)(2,1)S(1)}, u32[]{:S(2)}, u32[]{:S(2)}) collective-permute-start(bf16[4,5,80,128]{3,2,1,0:T(8,128)(2,1)S(1)} %get-tuple-element.14), channel_id=1, source_target_pairs={{1,0},{5,4},{9,8},{13,12},{17,16},{21,20},{25,24},{29,28},{0,1},{4... | collective-permute-start | bytes 1228808 | tf_op jit(solution)/shard_map/ppermute | solution.py:410
  21.6 0.0 copy-done.3
  21.6 0.0 copy-done.4
  21.6 13.0 %inner_rows.1 = (bf16[4,48,112,128]{3,2,1,0:T(8,128)(2,1)}, bf16[4,2,2,4,128,128]{5,4,3,2,1,0:T(8,128)(2,1)S(1)}) custom-call(bf16[4,5,2,4,112,128]{5,4,3,2,1,0:T(8,128)(2,1)S(1)} %first_rows.1.first_ref, bf16[4,3,80,128]{3,2,1,0:T(8,128)(2,1)S(1)} %get-tuple-element.11.west_ref, bf16[4,3,80,128]{3,2,1,0:T(8,128)(2,1)S(1)} %get-tuple-element.12.east_ref, ...), custom_call_target="tpu_custom_call" | custom-call | flops 7000000000 | bytes 12582912 | tf_op jit(solution)/shard_map/inner_rows/pallas_call | solution.py:352
  34.6 0.0 collective-permute-done.2.p_ref
  34.6 0.0 collective-permute-done.3.q_ref
  34.6 10.9 %outer_rows.1 = bf16[4,48,112,128]{3,2,1,0:T(8,128)(2,1)} custom-call(bf16[4,48,80,112]{3,2,1,0:T(8,128)(2,1)S(1)} %bitcast.7, bf16[4,48,80,112]{3,2,1,0:T(8,128)(2,1)S(1)} %bitcast.8, bf16[4,3,80,128]{3,2,1,0:T(8,128)(2,1)S(1)} %collective-permute-done.right_ref, ...), custom_call_target="tpu_custom_call", output_to_operand_aliasing={{}: (11, {})} | custom-call | flops 5000000000 | bytes 6291456 | tf_op jit(solution)/shard_map/outer_rows/pallas_call | solution.py:418
  (1 shorter events, 0.0 us)
Async XLA Ops:
  0.0 2.1 %copy-start = (bf16[4,48,112,80]{2,3,1,0:T(8,128)(2,1)S(1)}, bf16[4,48,112,80]{2,3,1,0:T(8,128)(2,1)}, u32[]{:S(2)}) copy-start(bf16[4,48,112,80]{2,3,1,0:T(8,128)(2,1)} %param.5) | copy-start | bytes 10321924
  2.1 5.6 %copy-start.1 = (bf16[4,48,112,80]{2,3,1,0:T(8,128)(2,1)S(1)}, bf16[4,48,112,80]{2,3,1,0:T(8,128)(2,1)}, u32[]{:S(2)}) copy-start(bf16[4,48,112,80]{2,3,1,0:T(8,128)(2,1)} %param.5) | copy-start | bytes 10321924
  2.1 5.6 %copy-start.2 = (bf16[3,3,128,128]{3,2,1,0:T(8,128)(2,1)S(1)}, bf16[3,3,128,128]{3,2,1,0:T(8,128)(2,1)}, u32[]{:S(2)}) copy-start(bf16[3,3,128,128]{3,2,1,0:T(8,128)(2,1)} %near_ref.5) | copy-start | bytes 884740
  2.1 5.6 %copy-start.5 = (bf16[80,128]{1,0:T(8,128)(2,1)S(1)}, bf16[80,128]{1,0:T(8,128)(2,1)}, u32[]{:S(2)}) copy-start(bf16[80,128]{1,0:T(8,128)(2,1)} %lift_ref.5) | copy-start | bytes 61444
  4.3 13.3 %collective-permute-start = (bf16[4,3,80,128]{3,2,1,0:T(8,128)(2,1)S(1)}, bf16[4,3,80,128]{3,2,1,0:T(8,128)(2,1)S(1)}, u32[]{:S(2)}, u32[]{:S(2)}) collective-permute-start(bf16[4,3,80,128]{3,2,1,0:T(8,128)(2,1)S(1)} %get-tuple-element.11.west_ref), channel_id=1, source_target_pairs={{4,0},{8,4},{12,8},{16,12},{20,16},{24,20},{28,24},{0,28},{5,1},{9... | collective-permute-start | bytes 737288 | tf_op jit(solution)/shard_map/ppermute | solution.py:388
  7.7 9.9 %collective-permute-start.1 = (bf16[4,3,80,128]{3,2,1,0:T(8,128)(2,1)S(1)}, bf16[4,3,80,128]{3,2,1,0:T(8,128)(2,1)S(1)}, u32[]{:S(2)}, u32[]{:S(2)}) collective-permute-start(bf16[4,3,80,128]{3,2,1,0:T(8,128)(2,1)S(1)} %get-tuple-element.12.east_ref), channel_id=1, source_target_pairs={{28,0},{0,4},{4,8},{8,12},{12,16},{16,20},{20,24},{24,28},{29,1},{... | collective-permute-start | bytes 737288 | tf_op jit(solution)/shard_map/ppermute | solution.py:389
  17.6 4.0 %copy-start.3 = (bf16[3,3,128,128]{3,2,1,0:T(8,128)(2,1)S(1)}, bf16[3,3,128,128]{3,2,1,0:T(8,128)(2,1)}, u32[]{:S(2)}) copy-start(bf16[3,3,128,128]{3,2,1,0:T(8,128)(2,1)} %far_ref.3) | copy-start | bytes 884740
  17.6 4.0 %copy-start.4 = (bf16[128,128]{1,0:T(8,128)(2,1)S(1)}, bf16[128,128]{1,0:T(8,128)(2,1)}, u32[]{:S(2)}) copy-start(bf16[128,128]{1,0:T(8,128)(2,1)} %mix_ref.3) | copy-start | bytes 98308
  18.4 16.2 %collective-permute-start.2 = (bf16[4,5,80,128]{3,2,1,0:T(8,128)(2,1)S(1)}, bf16[4,5,80,128]{3,2,1,0:T(8,128)(2,1)S(1)}, u32[]{:S(2)}, u32[]{:S(2)}) collective-permute-start(bf16[4,5,80,128]{3,2,1,0:T(8,128)(2,1)S(1)} %get-tuple-element.13), channel_id=1, source_target_pairs={{16,0},{20,4},{24,8},{28,12},{0,16},{4,20},{8,24},{12,28},{2,1},{6... | collective-permute-start | bytes 1228808 | tf_op jit(solution)/shard_map/ppermute | solution.py:409
  19.0 15.7 %collective-permute-start.3 = (bf16[4,5,80,128]{3,2,1,0:T(8,128)(2,1)S(1)}, bf16[4,5,80,128]{3,2,1,0:T(8,128)(2,1)S(1)}, u32[]{:S(2)}, u32[]{:S(2)}) collective-permute-start(bf16[4,5,80,128]{3,2,1,0:T(8,128)(2,1)S(1)} %get-tuple-element.14), channel_id=1, source_target_pairs={{1,0},{5,4},{9,8},{13,12},{17,16},{21,20},{25,24},{29,28},{0,1},{4... | collective-permute-start | bytes 1228808 | tf_op jit(solution)/shard_map/ppermute | solution.py:410

commit v3 on v2

--- a/solution.py
+++ b/solution.py
@@ -12,6 +12,7 @@
 F32 = jnp.float32
 HALO = 5
 SLOT = 8
+LAG = 1
 MIB = 1 << 20
 FIRST_MIB = 16
 INNER_MIB = 24
@@ -48,10 +49,16 @@
 
 
 def three_taps(row):
-    before = jnp.concatenate([row[:, 127:], row[:, :127]], axis=1)
-    after = jnp.concatenate([row[:, 1:], row[:, :1]], axis=1)
-    fill = jnp.zeros((256 - 3 * row.shape[0], 128), BF)
-    return jnp.concatenate([before, row, after, fill], axis=0).T
+    cin = row.shape[0]
+    fill = jnp.zeros((256 - 3 * cin, 128), BF)
+    tall = jnp.concatenate([row, row, row, fill], axis=0).T
+    lane = lax.broadcasted_iota(jnp.int32, (128, 128), 1)
+    low, high = tall[:, :128], tall[:, 128:]
+    before = jnp.concatenate([low[127:], low[:127]], axis=0)
+    after = jnp.concatenate([high[1:], high[:1]], axis=0)
+    low = jnp.where(lane < cin, before, low)
+    high = jnp.where(lane < 2 * cin - 128, high, after)
+    return jnp.concatenate([low, high], axis=1)
 
 
 def pack_columns(*refs):
@@ -60,12 +67,15 @@
     for group, x_ref in enumerate(x_refs):
         cols = x_ref.shape[3]
         rows = [widened(x_ref[0, i]) for i in range(x_ref.shape[1])]
-        for start, ref in ((0, west_ref), (cols - SLOT, east_ref)):
-            moved = [turned(row, i * SLOT - start) for i, row in enumerate(rows)]
-            packed = moved[0]
-            for i, row in enumerate(moved):
-                packed = jnp.where(lane < i * SLOT, packed, row)
-            ref[0, group] = packed
+        moved = [turned(row, i * SLOT) for i, row in enumerate(rows)]
+        offset = cols - SLOT
+        west, east = moved[0], moved[0]
+        for i, row in enumerate(moved):
+            west = jnp.where(lane < i * SLOT, west, row)
+            at = (i * SLOT + offset) % 128
+            east = jnp.where((lane >= at) & (lane < at + SLOT), row, east)
+        west_ref[0, group] = west
+        east_ref[0, group] = turned(east, -offset)
 
 
 def make_near(lift_ref, near_ref, wn_ref):
@@ -105,8 +115,9 @@
         q_ref[0, k] = jnp.where(even, bottom[k], top[k])
 
 
-def spread(f2, at, piece):
+def spread(f2, at, half, piece):
     inner = f2.shape[-2]
+    at = (*at, slice(None), slice(half * 128, half * 128 + 128))
     f2[(0, *at)] = jnp.concatenate([piece[128 - FAR :], piece[: inner - FAR]], axis=0)
     f2[(1, *at)] = piece[:inner]
     f2[(2, *at)] = piece[FAR : inner + FAR]
@@ -119,13 +130,12 @@
     return silu_of_half(dot(lhs, wn_ref[...].reshape(4 * 256, 256)))
 
 
-def far_block(f2, lead, g, wf_ref):
+def far_block(upper, lower, wf_ref):
     lhs = jnp.concatenate(
         [
-            jnp.concatenate([f2[(b, *lead, g + k, h, c)] for c in range(4)], axis=0)
+            jnp.concatenate([ref[(b, *at, c)] for c in range(4)], axis=0)
             for b in range(3)
-            for k in range(2)
-            for h in range(2)
+            for ref, at in (upper, lower)
         ],
         axis=1,
     )
@@ -137,21 +147,35 @@
     return [v[base : base + height, 128 * o : 128 * o + 128] for o in range(2)]
 
 
-def first_rows(x_ref, lift_ref, near_ref, first_ref, x3, wn_ref):
+def first_rows(x_ref, lift_ref, near_ref, first_ref, *scratch):
+    *x3s, wn_ref = scratch
+
     @pl.when(pl.program_id(0) == 0)
     def _():
         make_near(lift_ref, near_ref, wn_ref)
 
     cols = x_ref.shape[3]
-    for i in range(x3.shape[0]):
-        x3[i] = three_taps(widened(x_ref[0, i + FAR - 1]))[:cols]
-    for m in range(first_ref.shape[1]):
-        rows = [[x3[8 * m + 2 * p + i] for i in range(4)] for p in range(4)]
-        v = near_block(rows, wn_ref).astype(BF)
+    blocks = first_ref.shape[1]
+
+    def build(m):
+        for i in range(2 if m else 0, 10):
+            taps = three_taps(widened(x_ref[0, 8 * m + i + FAR - 1]))[:cols]
+            x3s[m][i] = taps
+            if i >= 8 and m + 1 < blocks:
+                x3s[m + 1][i - 8] = taps
+
+    def store(m, v):
         for p in range(4):
             for o, piece in enumerate(halves(v, p, cols)):
                 h, c = divmod(2 * p + o, 4)
                 first_ref[0, m, h, c] = piece
+
+    build(0)
+    for m in range(blocks):
+        rows = [[x3s[m][2 * p + i] for i in range(4)] for p in range(4)]
+        if m + 1 < blocks:
+            build(m + 1)
+        store(m, near_block(rows, wn_ref).astype(BF))
 
 
 def joined(main, strip):
@@ -166,15 +190,17 @@
 
 def inner_rows(
     first_ref, west_ref, east_ref, right_ref, left_ref, lift_ref, near_ref, far_ref, mix_ref,
-    out_ref, fx_ref, strips, f2, s, wn_ref, wf_ref, wm_ref,
+    out_ref, fx_ref, strips, *scratch
 ):
+    *f2s, s, wn_ref, wf_ref, wm_ref = scratch
+
     @pl.when(pl.program_id(0) == 0)
     def _():
         make_near(lift_ref, near_ref, wn_ref)
         make_far(far_ref, mix_ref, wf_ref, wm_ref)
 
-    blocks = f2.shape[1]
-    cols = f2.shape[-2]
+    blocks = len(f2s)
+    cols = f2s[0].shape[-2]
     per = 128 // SLOT
     lane = lax.rem(lax.broadcasted_iota(jnp.int32, (lift_ref.shape[0], 128), 1), SLOT)
     for g in range(west_ref.shape[1]):
@@ -188,19 +214,25 @@
     pairs = 4 * blocks
     rows = [[strips[low + 2 * q + i] for i in range(4)] for q in range(pairs)]
     v = near_block(rows, wn_ref)
-    for q in range(pairs):
-        m, p = divmod(q, 4)
-        for o, strip in enumerate(halves(v, q, 16)):
-            h, c = divmod(2 * p + o, 4)
-            piece = joined(first_ref[0, m, h, c], strip)
-            spread(f2, (m, h, c), piece)
-            if m == 0:
-                fx_ref[0, 0, h, c] = piece
-            if m == blocks - 1:
-                fx_ref[0, 1, h, c] = piece
     span = 4 * cols
-    for g in range(blocks - 1):
-        s[g * span : (g + 1) * span] = far_block(f2, (), g, wf_ref)
+
+    def far(g):
+        s[g * span : (g + 1) * span] = far_block((f2s[g], ()), (f2s[g + 1], ()), wf_ref)
+
+    for m in range(blocks):
+        for p in range(4):
+            for o, strip in enumerate(halves(v, 4 * m + p, 16)):
+                h, c = divmod(2 * p + o, 4)
+                piece = joined(first_ref[0, m, h, c], strip)
+                spread(f2s[m], (c,), h, piece)
+                if m == 0:
+                    fx_ref[0, 0, h, c] = piece
+                if m == blocks - 1:
+                    fx_ref[0, 1, h, c] = piece
+        if m >= LAG + 1:
+            far(m - 1 - LAG)
+    for g in range(blocks - 1 - LAG, blocks - 1):
+        far(g)
     y = dot(s[...], wm_ref[...]).astype(BF)
     for g in range(blocks - 1):
         for c in range(4):
@@ -210,7 +242,7 @@
 
 
 def outer_rows(
-    top_ref, bottom_ref, right_ref, left_ref, p_ref, q_ref, fx_ref,
+    p_own_ref, q_own_ref, p_ref, q_ref, fx_ref,
     lift_ref, near_ref, far_ref, mix_ref, _, out_ref,
     x3, f2, s, y, wn_ref, wf_ref, wm_ref, sems,
 ):
@@ -222,7 +254,7 @@
     cols = f2.shape[-2]
     total = out_ref.shape[1]
     span = 4 * cols
-    units = [(b, side) for b in range(top_ref.shape[0]) for side in range(2)]
+    units = [(b, side) for b in range(p_ref.shape[0]) for side in range(2)]
     for u, (b, side) in enumerate(units):
         pole = poles[side]
         moved = pole if side == 0 else jnp.logical_not(pole)
@@ -233,11 +265,8 @@
             taps = three_taps(jnp.where(from_p, p_ref[b, k], q_ref[b, k]))
             x3[u, base + k] = taps
         x3[u, 6 if side == 0 else 11] = x3[u, base + close]
-        own = top_ref if side == 0 else bottom_ref
         for k in range(HALO):
-            r = k if side == 0 else total - HALO + k
-            t = k if side == 0 else 8 - HALO + k
-            taps = three_taps(with_columns(own[b, t], right_ref, left_ref, b, r))
+            taps = three_taps(jnp.where(from_p, p_own_ref[b, k], q_own_ref[b, k]))
             x3[u, (7 if side == 0 else 6) + k] = taps
             if k == (0 if side == 0 else HALO - 1):
                 x3[u, jnp.where(moved, 0, HALO)] = taps
@@ -249,14 +278,14 @@
         for q in range(2):
             for o, piece in enumerate(halves(v, q, 128)):
                 c = 2 * q + o
-                spread(f2, (u, side, side, jnp.where(pole, 3 - c, c)), piece)
+                spread(f2, (u, side, jnp.where(pole, 3 - c, c)), side, piece)
             for o, piece in enumerate(halves(v, 2 + q, 128)):
-                spread(f2, (u, side, 1 - side, 2 * q + o), piece)
+                spread(f2, (u, side, 2 * q + o), 1 - side, piece)
         for h in range(2):
             for c in range(4):
-                spread(f2, (u, 1 - side, h, c), fx_ref[b, side, h, c])
+                spread(f2, (u, 1 - side, c), h, fx_ref[b, side, h, c])
     for u in range(len(units)):
-        s[u * span : (u + 1) * span] = far_block(f2, (u,), 0, wf_ref)
+        s[u * span : (u + 1) * span] = far_block((f2, (u, 0)), (f2, (u, 1)), wf_ref)
     copies = []
     for u, (b, side) in enumerate(units):
         done = dot(s[u * span : (u + 1) * span], wm_ref[...]).astype(BF)
@@ -338,7 +367,7 @@
         in_specs=[per_sample(x.shape)] + [whole(w.shape) for w in weights[:2]],
         out_specs=per_sample(first),
         out_shape=jax.ShapeDtypeStruct(first, BF),
-        scratch_shapes=[pltpu.VMEM((rows - 6, cols, 256), BF), made_weights()[0]],
+        scratch_shapes=[pltpu.VMEM((10, cols, 256), BF)] * (rows // 8 - 1) + [made_weights()[0]],
         compiler_params=params(FIRST_MIB),
         cost_estimate=cost(6 * 10**9, 9 * MIB),
         name="first_rows",
@@ -368,9 +397,9 @@
         ],
         scratch_shapes=[
             pltpu.VMEM((rows, 16, 256), BF),
-            pltpu.VMEM((3, blocks, 2, 4, cols, chan), BF),
-            pltpu.VMEM(((blocks - 1) * 4 * cols, 256), BF),
         ]
+        + [pltpu.VMEM((3, 4, cols, 256), BF)] * blocks
+        + [pltpu.VMEM(((blocks - 1) * 4 * cols, 256), BF)]
         + made_weights(),
         compiler_params=params(INNER_MIB),
         cost_estimate=cost(7 * 10**9, 12 * MIB),
@@ -413,12 +442,10 @@
     units = 2 * batch
     fx = edges.shape
     made = made_weights()
-    edge_rows = pl.BlockSpec((batch, 8, cin, cols), lambda i: (0, 0, 0, 0))
-    last_rows = pl.BlockSpec((batch, 8, cin, cols), lambda i: (0, last, 0, 0))
     return pl.pallas_call(
         outer_rows,
         grid=(1,),
-        in_specs=[edge_rows, last_rows, whole(edge), whole(edge), whole(strip), whole(strip)]
+        in_specs=[whole(strip)] * 4
         + [whole(fx)]
         + [whole(w.shape) for w in weights]
         + [pl.BlockSpec(memory_space=pl.ANY)],
@@ -426,17 +453,17 @@
         out_shape=jax.ShapeDtypeStruct((batch, rows, cols, chan), BF),
         scratch_shapes=[
             pltpu.VMEM((units, 12, 128, 256), BF),
-            pltpu.VMEM((3, units, 2, 2, 4, cols, chan), BF),
+            pltpu.VMEM((3, units, 2, 4, cols, 256), BF),
             pltpu.VMEM((units * 4 * cols, 256), BF),
             pltpu.VMEM((units, 8, cols, chan), BF),
         ]
         + made
         + [pltpu.SemaphoreType.DMA((units,))],
-        input_output_aliases={11: 0},
+        input_output_aliases={9: 0},
         compiler_params=params(OUTER_MIB),
         cost_estimate=cost(5 * 10**9, 6 * MIB),
         name="outer_rows",
-    )(x, x, right, left, p_got, q_got, edges, *weights, out)
+    )(p_send, q_send, p_got, q_got, edges, *weights, out)
 
 
 def solution(mesh):

time: 45.9 us -> 41.3 us (0.90)
  Pallas kernels: 36.7 us -> 31.2 us
  waiting for transfers between devices: 0.01 us -> 1.05 us
    pallas_call x1, Pallas kernels: 9.87 us -> 6.27 us  [call_first(): pl.pallas_call(first_rows, grid=(batch,), in_specs=[per_sample(x.shape)]...]
    pallas_call x1, Pallas kernels: 10.9 us -> 9.05 us  [on_device(): pl.pallas_call(outer_rows, grid=(1,), in_specs=[whole(strip)] * 4 + [whol...]
    ppermute x1, waiting for transfers between devices: 0.01 us -> 1.04 us  [on_device(): left = lax.ppermute(east, 'lon', [((i - 1) % lons, i) for i in range(lons)])]
  transfers between devices with their start and end apart: 4 -> 4, of which waited for: 0 -> 1; matrix products, arithmetic and copies ran while one was open for 0% -> 0% of each run, Pallas kernels for 50% -> 47%
where the time goes in v3:
time: 41.3 us; the launch traced here: 41.1 us
  Pallas kernels  31.2 us (76%)
  starting transfers between devices  6.57 us (16%)
  local copies, waits for them, and re-layouts  2.14 us (5%)
  waiting for transfers between devices  1.05 us (3%)
    pallas_call x1, Pallas kernels, call_inner(): pl.pallas_call(inner_rows, grid=(batch,), in_specs=[per_sample(first.shap...  13.1 us
    pallas_call x1, Pallas kernels, on_device(): pl.pallas_call(outer_rows, grid=(1,), in_specs=[whole(strip)] * 4 + [whol...  9.05 us
    pallas_call x1, Pallas kernels, call_first(): pl.pallas_call(first_rows, grid=(batch,), in_specs=[per_sample(x.shape)]...  6.27 us
    ppermute x1, starting transfers between devices, on_device(): lax.ppermute(west, 'lon', [((i + 1) % lons, i) for i in range(lons)])  3.35 us
    ppermute x1, starting transfers between devices, on_device(): q_got = lax.ppermute(q_send, ('lon', 'lat'), swaps(lats, lons, 0))  2.65 us
    unnamed x12, local copies, waits for them, and re-layouts  2.14 us
    pallas_call x1, Pallas kernels, call_pack(): pl.pallas_call(pack_columns, grid=(x.shape[0],), in_specs=[pl.BlockSpec((...  2.08 us
    ppermute x1, waiting for transfers between devices, on_device(): left = lax.ppermute(east, 'lon', [((i - 1) % lons, i) for i in range(lons)])  1.04 us
  transfers between devices with their start and end apart: 4, of which 1 were waited for; matrix products, arithmetic and copies ran while one was open for 0% of the time, Pallas kernels for 47%

profile of v3, /device:TPU:0, one launch (start us, length us, event | category | flops | bytes accessed | tf_op | source)
XLA Modules:
  0.0 41.1 jit_solution(8166309503762467467)
XLA Ops:
  0.0 0.0 copy-start
  0.0 2.1 %copy-done = bf16[4,48,112,80]{2,3,1,0:T(8,128)(2,1)S(1)} copy-done((bf16[4,48,112,80]{2,3,1,0:T(8,128)(2,1)S(1)}, bf16[4,48,112,80]{2,3,1,0:T(8,128)(2,1)}, u32[]{:S(2)}) %copy-start) | copy-done | bytes 3440664
  2.1 0.0 copy-start.1
  2.1 0.0 copy-start.2
  2.1 2.1 %pack_columns.1 = (bf16[4,3,80,128]{3,2,1,0:T(8,128)(2,1)S(1)}, bf16[4,3,80,128]{3,2,1,0:T(8,128)(2,1)S(1)}) custom-call(bf16[4,48,80,112]{3,2,1,0:T(8,128)(2,1)S(1)} %bitcast.1, bf16[4,48,80,112]{3,2,1,0:T(8,128)(2,1)S(1)} %bitcast.2, bf16[4,48,80,112]{3,2,1,0:T(8,128)(2,1)S(1)} %bitcast.3), custom_call_target="tpu_custom_call" | custom-call | bytes 4194304 | tf_op jit(solution)/shard_map/pack_columns/pallas_call | solution.py:343
  4.2 3.3 %collective-permute-start = (bf16[4,3,80,128]{3,2,1,0:T(8,128)(2,1)S(1)}, bf16[4,3,80,128]{3,2,1,0:T(8,128)(2,1)S(1)}, u32[]{:S(2)}, u32[]{:S(2)}) collective-permute-start(bf16[4,3,80,128]{3,2,1,0:T(8,128)(2,1)S(1)} %get-tuple-element.11.west_ref), channel_id=1, source_target_pairs={{4,0},{8,4},{12,8},{16,12},{20,16},{24,20},{28,24},{0,28},{5,1},{9... | collective-permute-start | bytes 737288 | tf_op jit(solution)/shard_map/ppermute | solution.py:417
  7.5 0.0 collective-permute-start.1
  7.6 0.0 copy-done.1
  7.6 0.0 copy-done.2
  7.6 0.0 copy-done.5
  7.6 6.3 %first_rows.1.first_ref = bf16[4,5,2,4,112,128]{5,4,3,2,1,0:T(8,128)(2,1)S(1)} custom-call(bf16[4,48,80,112]{3,2,1,0:T(8,128)(2,1)S(1)} %bitcast.4, bf16[80,128]{1,0:T(8,128)(2,1)S(1)} %copy-done.5, bf16[3,3,128,128]{3,2,1,0:T(8,128)(2,1)S(1)} %copy-done.2), custom_call_target="tpu_custom_call" | custom-call | flops 6000000000 | bytes 9437184 | tf_op jit(solution)/shard_map/first_rows/pallas_call | solution.py:364
  13.8 0.0 copy-start.3
  13.9 0.0 copy-start.4
  13.9 0.0 collective-permute-done.right_ref
  13.9 1.0 %collective-permute-done.1.left_ref = bf16[4,3,80,128]{3,2,1,0:T(8,128)(2,1)S(1)} collective-permute-done((bf16[4,3,80,128]{3,2,1,0:T(8,128)(2,1)S(1)}, bf16[4,3,80,128]{3,2,1,0:T(8,128)(2,1)S(1)}, u32[]{:S(2)}, u32[]{:S(2)}) %collective-permute-start.1) | collective-permute-done | bytes 245792 | tf_op jit(solution)/shard_map/ppermute | solution.py:418
  14.9 0.7 %pack_rows.1 = (bf16[4,5,80,128]{3,2,1,0:T(8,128)(2,1)S(1)}, bf16[4,5,80,128]{3,2,1,0:T(8,128)(2,1)S(1)}) custom-call(bf16[4,48,80,112]{3,2,1,0:T(8,128)(2,1)S(1)} %bitcast.5, bf16[4,48,80,112]{3,2,1,0:T(8,128)(2,1)S(1)} %bitcast.6, bf16[4,3,80,128]{3,2,1,0:T(8,128)(2,1)S(1)} %collective-permute-done.right_ref, ...), custom_call_target="tpu_custom_call" | custom-call | bytes 2097152 | tf_op jit(solution)/shard_map/pack_rows/pallas_call | solution.py:423
  15.6 0.6 %collective-permute-start.2 = (bf16[4,5,80,128]{3,2,1,0:T(8,128)(2,1)S(1)}, bf16[4,5,80,128]{3,2,1,0:T(8,128)(2,1)S(1)}, u32[]{:S(2)}, u32[]{:S(2)}) collective-permute-start(bf16[4,5,80,128]{3,2,1,0:T(8,128)(2,1)S(1)} %get-tuple-element.13.p_own_ref), channel_id=1, source_target_pairs={{16,0},{20,4},{24,8},{28,12},{0,16},{4,20},{8,24},{12,28},{2,1},{6... | collective-permute-start | bytes 1228808 | tf_op jit(solution)/shard_map/ppermute | solution.py:438
  16.2 2.6 %collective-permute-start.3 = (bf16[4,5,80,128]{3,2,1,0:T(8,128)(2,1)S(1)}, bf16[4,5,80,128]{3,2,1,0:T(8,128)(2,1)S(1)}, u32[]{:S(2)}, u32[]{:S(2)}) collective-permute-start(bf16[4,5,80,128]{3,2,1,0:T(8,128)(2,1)S(1)} %get-tuple-element.14.q_own_ref), channel_id=1, source_target_pairs={{1,0},{5,4},{9,8},{13,12},{17,16},{21,20},{25,24},{29,28},{0,1},{4... | collective-permute-start | bytes 1228808 | tf_op jit(solution)/shard_map/ppermute | solution.py:439
  18.9 0.0 copy-done.3
  18.9 0.0 copy-done.4
  18.9 13.1 %inner_rows.1 = (bf16[4,48,112,128]{3,2,1,0:T(8,128)(2,1)}, bf16[4,2,2,4,128,128]{5,4,3,2,1,0:T(8,128)(2,1)S(1)}) custom-call(bf16[4,5,2,4,112,128]{5,4,3,2,1,0:T(8,128)(2,1)S(1)} %first_rows.1.first_ref, bf16[4,3,80,128]{3,2,1,0:T(8,128)(2,1)S(1)} %get-tuple-element.11.west_ref, bf16[4,3,80,128]{3,2,1,0:T(8,128)(2,1)S(1)} %get-tuple-element.12.east_ref, ...), custom_call_target="tpu_custom_call" | custom-call | flops 7000000000 | bytes 12582912 | tf_op jit(solution)/shard_map/inner_rows/pallas_call | solution.py:381
  31.9 0.0 collective-permute-done.2.p_ref
  31.9 0.0 collective-permute-done.3.q_ref
  31.9 9.1 %outer_rows.1 = bf16[4,48,112,128]{3,2,1,0:T(8,128)(2,1)} custom-call(bf16[4,5,80,128]{3,2,1,0:T(8,128)(2,1)S(1)} %get-tuple-element.13.p_own_ref, bf16[4,5,80,128]{3,2,1,0:T(8,128)(2,1)S(1)} %get-tuple-element.14.q_own_ref, bf16[4,5,80,128]{3,2,1,0:T(8,128)(2,1)S(1)} %collective-permute-done.2.p_ref, ...), custom_call_target="tpu_custom_call", output_to_operand_aliasing={{}: (9, {})} | custom-call | flops 5000000000 | bytes 6291456 | tf_op jit(solution)/shard_map/outer_rows/pallas_call | solution.py:445
  (1 shorter events, 0.0 us)
Async XLA Ops:
  0.0 2.1 %copy-start = (bf16[4,48,112,80]{2,3,1,0:T(8,128)(2,1)S(1)}, bf16[4,48,112,80]{2,3,1,0:T(8,128)(2,1)}, u32[]{:S(2)}) copy-start(bf16[4,48,112,80]{2,3,1,0:T(8,128)(2,1)} %param.5) | copy-start | bytes 10321924
  2.1 5.4 %copy-start.1 = (bf16[4,48,112,80]{2,3,1,0:T(8,128)(2,1)S(1)}, bf16[4,48,112,80]{2,3,1,0:T(8,128)(2,1)}, u32[]{:S(2)}) copy-start(bf16[4,48,112,80]{2,3,1,0:T(8,128)(2,1)} %param.5) | copy-start | bytes 10321924
  2.1 5.4 %copy-start.2 = (bf16[3,3,128,128]{3,2,1,0:T(8,128)(2,1)S(1)}, bf16[3,3,128,128]{3,2,1,0:T(8,128)(2,1)}, u32[]{:S(2)}) copy-start(bf16[3,3,128,128]{3,2,1,0:T(8,128)(2,1)} %near_ref.5) | copy-start | bytes 884740
  2.1 5.4 %copy-start.5 = (bf16[80,128]{1,0:T(8,128)(2,1)S(1)}, bf16[80,128]{1,0:T(8,128)(2,1)}, u32[]{:S(2)}) copy-start(bf16[80,128]{1,0:T(8,128)(2,1)} %lift_ref.5) | copy-start | bytes 61444
  4.2 9.7 %collective-permute-start = (bf16[4,3,80,128]{3,2,1,0:T(8,128)(2,1)S(1)}, bf16[4,3,80,128]{3,2,1,0:T(8,128)(2,1)S(1)}, u32[]{:S(2)}, u32[]{:S(2)}) collective-permute-start(bf16[4,3,80,128]{3,2,1,0:T(8,128)(2,1)S(1)} %get-tuple-element.11.west_ref), channel_id=1, source_target_pairs={{4,0},{8,4},{12,8},{16,12},{20,16},{24,20},{28,24},{0,28},{5,1},{9... | collective-permute-start | bytes 737288 | tf_op jit(solution)/shard_map/ppermute | solution.py:417
  7.5 7.4 %collective-permute-start.1 = (bf16[4,3,80,128]{3,2,1,0:T(8,128)(2,1)S(1)}, bf16[4,3,80,128]{3,2,1,0:T(8,128)(2,1)S(1)}, u32[]{:S(2)}, u32[]{:S(2)}) collective-permute-start(bf16[4,3,80,128]{3,2,1,0:T(8,128)(2,1)S(1)} %get-tuple-element.12.east_ref), channel_id=1, source_target_pairs={{28,0},{0,4},{4,8},{8,12},{12,16},{16,20},{20,24},{24,28},{29,1},{... | collective-permute-start | bytes 737288 | tf_op jit(solution)/shard_map/ppermute | solution.py:418
  13.8 5.0 %copy-start.3 = (bf16[3,3,128,128]{3,2,1,0:T(8,128)(2,1)S(1)}, bf16[3,3,128,128]{3,2,1,0:T(8,128)(2,1)}, u32[]{:S(2)}) copy-start(bf16[3,3,128,128]{3,2,1,0:T(8,128)(2,1)} %far_ref.3) | copy-start | bytes 884740
  13.9 5.0 %copy-start.4 = (bf16[128,128]{1,0:T(8,128)(2,1)S(1)}, bf16[128,128]{1,0:T(8,128)(2,1)}, u32[]{:S(2)}) copy-start(bf16[128,128]{1,0:T(8,128)(2,1)} %mix_ref.3) | copy-start | bytes 98308
  15.6 16.3 %collective-permute-start.2 = (bf16[4,5,80,128]{3,2,1,0:T(8,128)(2,1)S(1)}, bf16[4,5,80,128]{3,2,1,0:T(8,128)(2,1)S(1)}, u32[]{:S(2)}, u32[]{:S(2)}) collective-permute-start(bf16[4,5,80,128]{3,2,1,0:T(8,128)(2,1)S(1)} %get-tuple-element.13.p_own_ref), channel_id=1, source_target_pairs={{16,0},{20,4},{24,8},{28,12},{0,16},{4,20},{8,24},{12,28},{2,1},{6... | collective-permute-start | bytes 1228808 | tf_op jit(solution)/shard_map/ppermute | solution.py:438
  16.2 15.7 %collective-permute-start.3 = (bf16[4,5,80,128]{3,2,1,0:T(8,128)(2,1)S(1)}, bf16[4,5,80,128]{3,2,1,0:T(8,128)(2,1)S(1)}, u32[]{:S(2)}, u32[]{:S(2)}) collective-permute-start(bf16[4,5,80,128]{3,2,1,0:T(8,128)(2,1)S(1)} %get-tuple-element.14.q_own_ref), channel_id=1, source_target_pairs={{1,0},{5,4},{9,8},{13,12},{17,16},{21,20},{25,24},{29,28},{0,1},{4... | collective-permute-start | bytes 1228808 | tf_op jit(solution)/shard_map/ppermute | solution.py:439

commit v4 on v3

--- a/solution.py
+++ b/solution.py
@@ -12,8 +12,10 @@
 F32 = jnp.float32
 HALO = 5
 SLOT = 8
-LAG = 1
+WIDE = 1
+EVERY = 4
 MIB = 1 << 20
+MADE = ((4, 256, 256), (6 * 256, 256), (256, 256))
 FIRST_MIB = 16
 INNER_MIB = 24
 OUTER_MIB = 34
@@ -116,11 +118,13 @@
 
 
 def spread(f2, at, half, piece):
-    inner = f2.shape[-2]
-    at = (*at, slice(None), slice(half * 128, half * 128 + 128))
-    f2[(0, *at)] = jnp.concatenate([piece[128 - FAR :], piece[: inner - FAR]], axis=0)
-    f2[(1, *at)] = piece[:inner]
-    f2[(2, *at)] = piece[FAR : inner + FAR]
+    turned_piece = jnp.concatenate([piece[128 - FAR :], piece[: 128 - FAR]], axis=0)
+    f2[(*at, slice(None), slice(half * 128, half * 128 + 128))] = turned_piece
+
+
+def tap(ref, b, at, c):
+    cols = ref.shape[-2] - 16
+    return ref[(*at, c, slice(b * FAR, b * FAR + cols))]
 
 
 def near_block(rows, wn_ref):
@@ -130,12 +134,12 @@
     return silu_of_half(dot(lhs, wn_ref[...].reshape(4 * 256, 256)))
 
 
-def far_block(upper, lower, wf_ref):
+def far_block(uppers, lowers, wf_ref):
     lhs = jnp.concatenate(
         [
-            jnp.concatenate([ref[(b, *at, c)] for c in range(4)], axis=0)
+            jnp.concatenate([tap(ref, b, at, c) for ref, at in refs for c in range(4)], axis=0)
             for b in range(3)
-            for ref, at in (upper, lower)
+            for refs in (uppers, lowers)
         ],
         axis=1,
     )
@@ -147,8 +151,7 @@
     return [v[base : base + height, 128 * o : 128 * o + 128] for o in range(2)]
 
 
-def first_rows(x_ref, lift_ref, near_ref, first_ref, *scratch):
-    *x3s, wn_ref = scratch
+def first_rows(x_ref, lift_ref, near_ref, first_ref, wn_ref, *x3s):
 
     @pl.when(pl.program_id(0) == 0)
     def _():
@@ -188,40 +191,49 @@
     )
 
 
-def inner_rows(
-    first_ref, west_ref, east_ref, right_ref, left_ref, lift_ref, near_ref, far_ref, mix_ref,
-    out_ref, fx_ref, strips, *scratch
-):
-    *f2s, s, wn_ref, wf_ref, wm_ref = scratch
-
-    @pl.when(pl.program_id(0) == 0)
-    def _():
-        make_near(lift_ref, near_ref, wn_ref)
-        make_far(far_ref, mix_ref, wf_ref, wm_ref)
-
-    blocks = len(f2s)
-    cols = f2s[0].shape[-2]
+def edge_strips(b, west_ref, east_ref, right_ref, left_ref, wn_ref, strips, pairs):
+    cin = west_ref.shape[2]
     per = 128 // SLOT
-    lane = lax.rem(lax.broadcasted_iota(jnp.int32, (lift_ref.shape[0], 128), 1), SLOT)
+    lane = lax.rem(lax.broadcasted_iota(jnp.int32, (cin, 128), 1), SLOT)
     for g in range(west_ref.shape[1]):
-        right = jnp.where(lane < 2, turned(east_ref[0, g], -6), turned(right_ref[0, g], 2))
-        left = jnp.where(lane < 6, turned(left_ref[0, g], -2), turned(west_ref[0, g], 6))
+        right = jnp.where(lane < 2, turned(east_ref[b, g], -6), turned(right_ref[b, g], 2))
+        left = jnp.where(lane < 6, turned(left_ref[b, g], -2), turned(west_ref[b, g], 6))
         right, left = three_taps(right), three_taps(left)
         for i in range(per):
             at = slice(SLOT * i, SLOT * i + SLOT)
-            strips[per * g + i] = jnp.concatenate([right[at], left[at]], axis=0)
+            strips[b, per * g + i] = jnp.concatenate([right[at], left[at]], axis=0)
     low = FAR - 1
+    rows = [[strips[b, low + 2 * q + i] for i in range(4)] for q in range(pairs)]
+    return near_block(rows, wn_ref)
+
+
+def inner_rows(
+    first_ref, west_ref, east_ref, right_ref, left_ref, wn_ref, far_ref, mix_ref,
+    out_ref, fx_ref, wf_ref, wm_ref, strips, edge, s, *f2s,
+):
+    blocks = len(f2s)
+    cols = f2s[0].shape[-2] - 16
     pairs = 4 * blocks
-    rows = [[strips[low + 2 * q + i] for i in range(4)] for q in range(pairs)]
-    v = near_block(rows, wn_ref)
+
+    @pl.when(pl.program_id(0) == 0)
+    def _():
+        make_far(far_ref, mix_ref, wf_ref, wm_ref)
+        for b in range(west_ref.shape[0]):
+            edge[b] = edge_strips(
+                b, west_ref, east_ref, right_ref, left_ref, wn_ref, strips, pairs
+            )
+
+    sample = pl.program_id(0)
     span = 4 * cols
 
     def far(g):
-        s[g * span : (g + 1) * span] = far_block((f2s[g], ()), (f2s[g + 1], ()), wf_ref)
+        near, next_ = ([(f2s[i + k], ()) for i in range(g, g + WIDE)] for k in range(2))
+        s[g * span : (g + WIDE) * span] = far_block(near, next_, wf_ref)
 
     for m in range(blocks):
         for p in range(4):
-            for o, strip in enumerate(halves(v, 4 * m + p, 16)):
+            q = 4 * m + p
+            for o, strip in enumerate(halves(edge[sample, 16 * q : 16 * q + 16], 0, 16)):
                 h, c = divmod(2 * p + o, 4)
                 piece = joined(first_ref[0, m, h, c], strip)
                 spread(f2s[m], (c,), h, piece)
@@ -229,10 +241,8 @@
                     fx_ref[0, 0, h, c] = piece
                 if m == blocks - 1:
                     fx_ref[0, 1, h, c] = piece
-        if m >= LAG + 1:
-            far(m - 1 - LAG)
-    for g in range(blocks - 1 - LAG, blocks - 1):
-        far(g)
+        if m >= WIDE and (m - WIDE) % WIDE == 0:
+            far(m - WIDE)
     y = dot(s[...], wm_ref[...]).astype(BF)
     for g in range(blocks - 1):
         for c in range(4):
@@ -243,15 +253,12 @@
 
 def outer_rows(
     p_own_ref, q_own_ref, p_ref, q_ref, fx_ref,
-    lift_ref, near_ref, far_ref, mix_ref, _, out_ref,
-    x3, f2, s, y, wn_ref, wf_ref, wm_ref, sems,
+    wn_ref, wf_ref, wm_ref, _, out_ref, x3, f2, s, y, sems,
 ):
-    make_near(lift_ref, near_ref, wn_ref)
-    make_far(far_ref, mix_ref, wf_ref, wm_ref)
     lat = lax.axis_index("lat")
     even = lax.rem(lat, 2) == 0
     poles = (lat == 0, lat == lax.axis_size("lat") - 1)
-    cols = f2.shape[-2]
+    cols = f2.shape[-2] - 16
     total = out_ref.shape[1]
     span = 4 * cols
     units = [(b, side) for b in range(p_ref.shape[0]) for side in range(2)]
@@ -284,10 +291,10 @@
         for h in range(2):
             for c in range(4):
                 spread(f2, (u, 1 - side, c), h, fx_ref[b, side, h, c])
-    for u in range(len(units)):
-        s[u * span : (u + 1) * span] = far_block((f2, (u, 0)), (f2, (u, 1)), wf_ref)
     copies = []
-    for u, (b, side) in enumerate(units):
+
+    def finish(u):
+        b, side = units[u]
         done = dot(s[u * span : (u + 1) * span], wm_ref[...]).astype(BF)
         for c in range(4):
             for h in range(2):
@@ -296,6 +303,12 @@
         copy = pltpu.make_async_copy(y.at[u], to, sems.at[u])
         copy.start()
         copies.append(copy)
+
+    for u in range(len(units)):
+        s[u * span : (u + 1) * span] = far_block([(f2, (u, 0))], [(f2, (u, 1))], wf_ref)
+        if (u + 1) % EVERY == 0:
+            for done_unit in range(u + 1 - EVERY, u + 1):
+                finish(done_unit)
     for copy in copies:
         copy.wait()
 
@@ -329,10 +342,6 @@
     return pairs
 
 
-def made_weights():
-    return [pltpu.VMEM(shape, BF) for shape in ((4, 256, 256), (6 * 256, 256), (256, 256))]
-
-
 def edge_shape(x):
     per = 128 // SLOT
     return (x.shape[0], -(-x.shape[1] // per), x.shape[2], 128)
@@ -365,16 +374,16 @@
         first_rows,
         grid=(batch,),
         in_specs=[per_sample(x.shape)] + [whole(w.shape) for w in weights[:2]],
-        out_specs=per_sample(first),
-        out_shape=jax.ShapeDtypeStruct(first, BF),
-        scratch_shapes=[pltpu.VMEM((10, cols, 256), BF)] * (rows // 8 - 1) + [made_weights()[0]],
+        out_specs=[per_sample(first), whole(MADE[0])],
+        out_shape=[jax.ShapeDtypeStruct(shape, BF) for shape in (first, MADE[0])],
+        scratch_shapes=[pltpu.VMEM((10, cols, 256), BF)] * (rows // 8 - 1),
         compiler_params=params(FIRST_MIB),
         cost_estimate=cost(6 * 10**9, 9 * MIB),
         name="first_rows",
     )(x, *weights[:2])
 
 
-def call_inner(first, west, east, right, left, weights, rows):
+def call_inner(first, wn, west, east, right, left, weights, rows):
     batch, blocks, _, _, cols, chan = first.shape
     fx = (batch, 2, 2, 4, 128, chan)
     inner = rows - 16
@@ -382,29 +391,31 @@
         inner_rows,
         grid=(batch,),
         in_specs=[per_sample(first.shape)]
-        + [per_sample(right.shape)] * 4
-        + [whole(w.shape) for w in weights],
+        + [whole(right.shape)] * 4
+        + [whole(w.shape) for w in (wn, *weights[2:])],
         out_specs=[
             pl.BlockSpec(
                 (pl.Element(1), pl.Element(inner), pl.Element(cols), pl.Element(chan)),
                 lambda b: (b, 8, 0, 0),
             ),
             per_sample(fx),
+            whole(MADE[1]),
+            whole(MADE[2]),
         ],
         out_shape=[
-            jax.ShapeDtypeStruct((batch, rows, cols, chan), BF),
-            jax.ShapeDtypeStruct(fx, BF),
+            jax.ShapeDtypeStruct(shape, BF)
+            for shape in ((batch, rows, cols, chan), fx, MADE[1], MADE[2])
         ],
         scratch_shapes=[
-            pltpu.VMEM((rows, 16, 256), BF),
+            pltpu.VMEM((batch, rows, 16, 256), BF),
+            pltpu.VMEM((batch, 16 * 4 * blocks, 256), F32),
+            pltpu.VMEM(((blocks - 1) * 4 * cols, 256), BF),
         ]
-        + [pltpu.VMEM((3, 4, cols, 256), BF)] * blocks
-        + [pltpu.VMEM(((blocks - 1) * 4 * cols, 256), BF)]
-        + made_weights(),
+        + [pltpu.VMEM((4, cols + 16, 256), BF)] * blocks,
         compiler_params=params(INNER_MIB),
         cost_estimate=cost(7 * 10**9, 12 * MIB),
         name="inner_rows",
-    )(first, west, east, right, left, *weights)
+    )(first, west, east, right, left, wn, *weights[2:])
 
 
 def on_device(fields, lift_weight, near_kernel, far_kernel, mix_weight):
@@ -417,7 +428,7 @@
     right = lax.ppermute(west, "lon", [((i + 1) % lons, i) for i in range(lons)])
     left = lax.ppermute(east, "lon", [((i - 1) % lons, i) for i in range(lons)])
     weights = (lift_weight, near_kernel, far_kernel, mix_weight)
-    first = call_first(x, weights)
+    first, wn = call_first(x, weights)
     strip = (batch, HALO, cin, 128)
     last = rows // 8 - 1
     p_send, q_send = pl.pallas_call(
@@ -438,32 +449,30 @@
     p_got = lax.ppermute(p_send, ("lon", "lat"), swaps(lats, lons, 1))
     q_got = lax.ppermute(q_send, ("lon", "lat"), swaps(lats, lons, 0))
 
-    out, edges = call_inner(first, west, east, right, left, weights, rows)
+    out, edges, wf, wm = call_inner(first, wn, west, east, right, left, weights, rows)
     units = 2 * batch
     fx = edges.shape
-    made = made_weights()
     return pl.pallas_call(
         outer_rows,
         grid=(1,),
         in_specs=[whole(strip)] * 4
         + [whole(fx)]
-        + [whole(w.shape) for w in weights]
+        + [whole(shape) for shape in MADE]
         + [pl.BlockSpec(memory_space=pl.ANY)],
         out_specs=pl.BlockSpec(memory_space=pl.ANY),
         out_shape=jax.ShapeDtypeStruct((batch, rows, cols, chan), BF),
         scratch_shapes=[
             pltpu.VMEM((units, 12, 128, 256), BF),
-            pltpu.VMEM((3, units, 2, 4, cols, 256), BF),
+            pltpu.VMEM((units, 2, 4, cols + 16, 256), BF),
             pltpu.VMEM((units * 4 * cols, 256), BF),
             pltpu.VMEM((units, 8, cols, chan), BF),
-        ]
-        + made
-        + [pltpu.SemaphoreType.DMA((units,))],
-        input_output_aliases={9: 0},
+            pltpu.SemaphoreType.DMA((units,)),
+        ],
+        input_output_aliases={8: 0},
         compiler_params=params(OUTER_MIB),
         cost_estimate=cost(5 * 10**9, 6 * MIB),
         name="outer_rows",
-    )(p_send, q_send, p_got, q_got, edges, *weights, out)
+    )(p_send, q_send, p_got, q_got, edges, wn, wf, wm, out)
 
 
 def solution(mesh):

time: 41.3 us -> 36.8 us (0.89)
  Pallas kernels: 31.2 us -> 26.8 us
    pallas_call x1, Pallas kernels: 13.1 us -> 9.96 us  [call_inner(): pl.pallas_call(inner_rows, grid=(batch,), in_specs=[per_sample(first.shap...]
    pallas_call x1, Pallas kernels: 9.05 us -> 7.83 us  [on_device(): pl.pallas_call(outer_rows, grid=(1,), in_specs=[whole(strip)] * 4 + [whol...]
  transfers between devices with their start and end apart: 4 -> 4, of which waited for: 1 -> 1; matrix products, arithmetic and copies ran while one was open for 0% -> 0% of each run, Pallas kernels for 47% -> 44%
where the time goes in v4:
time: 36.8 us; the launch traced here: 36.7 us
  Pallas kernels  26.8 us (73%)
  starting transfers between devices  6.57 us (18%)
  local copies, waits for them, and re-layouts  2.14 us (6%)
  waiting for transfers between devices  1.04 us (3%)
    pallas_call x1, Pallas kernels, call_inner(): pl.pallas_call(inner_rows, grid=(batch,), in_specs=[per_sample(first.shap...  9.96 us
    pallas_call x1, Pallas kernels, on_device(): pl.pallas_call(outer_rows, grid=(1,), in_specs=[whole(strip)] * 4 + [whol...  7.83 us
    pallas_call x1, Pallas kernels, call_first(): pl.pallas_call(first_rows, grid=(batch,), in_specs=[per_sample(x.shape)]...  6.27 us
    ppermute x1, starting transfers between devices, on_device(): lax.ppermute(west, 'lon', [((i + 1) % lons, i) for i in range(lons)])  3.35 us
    ppermute x1, starting transfers between devices, on_device(): q_got = lax.ppermute(q_send, ('lon', 'lat'), swaps(lats, lons, 0))  2.65 us
    unnamed x12, local copies, waits for them, and re-layouts  2.14 us
    pallas_call x1, Pallas kernels, call_pack(): pl.pallas_call(pack_columns, grid=(x.shape[0],), in_specs=[pl.BlockSpec((...  2.08 us
    ppermute x1, waiting for transfers between devices, on_device(): left = lax.ppermute(east, 'lon', [((i - 1) % lons, i) for i in range(lons)])  1.04 us
  transfers between devices with their start and end apart: 4, of which 1 were waited for; matrix products, arithmetic and copies ran while one was open for 0% of the time, Pallas kernels for 44%

profile of v4, /device:TPU:0, one launch (start us, length us, event | category | flops | bytes accessed | tf_op | source)
XLA Modules:
  0.0 36.7 jit_solution(2739650335419951642)
XLA Ops:
  0.0 0.0 copy-start
  0.0 2.1 %copy-done = bf16[4,48,112,80]{2,3,1,0:T(8,128)(2,1)S(1)} copy-done((bf16[4,48,112,80]{2,3,1,0:T(8,128)(2,1)S(1)}, bf16[4,48,112,80]{2,3,1,0:T(8,128)(2,1)}, u32[]{:S(2)}) %copy-start) | copy-done | bytes 3440664
  2.1 0.0 copy-start.1
  2.1 0.0 copy-start.2
  2.1 2.1 %pack_columns.1 = (bf16[4,3,80,128]{3,2,1,0:T(8,128)(2,1)S(1)}, bf16[4,3,80,128]{3,2,1,0:T(8,128)(2,1)S(1)}) custom-call(bf16[4,48,80,112]{3,2,1,0:T(8,128)(2,1)S(1)} %bitcast.1, bf16[4,48,80,112]{3,2,1,0:T(8,128)(2,1)S(1)} %bitcast.2, bf16[4,48,80,112]{3,2,1,0:T(8,128)(2,1)S(1)} %bitcast.3), custom_call_target="tpu_custom_call" | custom-call | bytes 4194304 | tf_op jit(solution)/shard_map/pack_columns/pallas_call | solution.py:352
  4.2 3.3 %collective-permute-start = (bf16[4,3,80,128]{3,2,1,0:T(8,128)(2,1)S(1)}, bf16[4,3,80,128]{3,2,1,0:T(8,128)(2,1)S(1)}, u32[]{:S(2)}, u32[]{:S(2)}) collective-permute-start(bf16[4,3,80,128]{3,2,1,0:T(8,128)(2,1)S(1)} %get-tuple-element.15.west_ref), channel_id=1, source_target_pairs={{4,0},{8,4},{12,8},{16,12},{20,16},{24,20},{28,24},{0,28},{5,1},{9... | collective-permute-start | bytes 737288 | tf_op jit(solution)/shard_map/ppermute | solution.py:428
  7.5 0.0 collective-permute-start.1
  7.6 0.0 copy-done.1
  7.6 0.0 copy-done.2
  7.6 0.0 copy-done.5
  7.6 6.3 %first_rows.1 = (bf16[4,5,2,4,112,128]{5,4,3,2,1,0:T(8,128)(2,1)S(1)}, bf16[4,256,256]{2,1,0:T(8,128)(2,1)S(1)}) custom-call(bf16[4,48,80,112]{3,2,1,0:T(8,128)(2,1)S(1)} %bitcast.4, bf16[80,128]{1,0:T(8,128)(2,1)S(1)} %copy-done.5, bf16[3,3,128,128]{3,2,1,0:T(8,128)(2,1)S(1)} %copy-done.2), custom_call_target="tpu_custom_call" | custom-call | flops 6000000000 | bytes 9437184 | tf_op jit(solution)/shard_map/first_rows/pallas_call | solution.py:373
  13.8 0.0 copy-start.3
  13.9 0.0 copy-start.4
  13.9 0.0 collective-permute-done.right_ref
  13.9 1.0 %collective-permute-done.1.left_ref = bf16[4,3,80,128]{3,2,1,0:T(8,128)(2,1)S(1)} collective-permute-done((bf16[4,3,80,128]{3,2,1,0:T(8,128)(2,1)S(1)}, bf16[4,3,80,128]{3,2,1,0:T(8,128)(2,1)S(1)}, u32[]{:S(2)}, u32[]{:S(2)}) %collective-permute-start.1) | collective-permute-done | bytes 245792 | tf_op jit(solution)/shard_map/ppermute | solution.py:429
  14.9 0.7 %pack_rows.1 = (bf16[4,5,80,128]{3,2,1,0:T(8,128)(2,1)S(1)}, bf16[4,5,80,128]{3,2,1,0:T(8,128)(2,1)S(1)}) custom-call(bf16[4,48,80,112]{3,2,1,0:T(8,128)(2,1)S(1)} %bitcast.5, bf16[4,48,80,112]{3,2,1,0:T(8,128)(2,1)S(1)} %bitcast.6, bf16[4,3,80,128]{3,2,1,0:T(8,128)(2,1)S(1)} %collective-permute-done.right_ref, ...), custom_call_target="tpu_custom_call" | custom-call | bytes 2097152 | tf_op jit(solution)/shard_map/pack_rows/pallas_call | solution.py:434
  15.6 0.6 %collective-permute-start.2 = (bf16[4,5,80,128]{3,2,1,0:T(8,128)(2,1)S(1)}, bf16[4,5,80,128]{3,2,1,0:T(8,128)(2,1)S(1)}, u32[]{:S(2)}, u32[]{:S(2)}) collective-permute-start(bf16[4,5,80,128]{3,2,1,0:T(8,128)(2,1)S(1)} %get-tuple-element.17.p_own_ref), channel_id=1, source_target_pairs={{16,0},{20,4},{24,8},{28,12},{0,16},{4,20},{8,24},{12,28},{2,1},{6... | collective-permute-start | bytes 1228808 | tf_op jit(solution)/shard_map/ppermute | solution.py:449
  16.2 2.6 %collective-permute-start.3 = (bf16[4,5,80,128]{3,2,1,0:T(8,128)(2,1)S(1)}, bf16[4,5,80,128]{3,2,1,0:T(8,128)(2,1)S(1)}, u32[]{:S(2)}, u32[]{:S(2)}) collective-permute-start(bf16[4,5,80,128]{3,2,1,0:T(8,128)(2,1)S(1)} %get-tuple-element.18.q_own_ref), channel_id=1, source_target_pairs={{1,0},{5,4},{9,8},{13,12},{17,16},{21,20},{25,24},{29,28},{0,1},{4... | collective-permute-start | bytes 1228808 | tf_op jit(solution)/shard_map/ppermute | solution.py:450
  18.9 0.0 copy-done.3
  18.9 0.0 copy-done.4
  18.9 10.0 %inner_rows.1 = (bf16[4,48,112,128]{3,2,1,0:T(8,128)(2,1)}, bf16[4,2,2,4,128,128]{5,4,3,2,1,0:T(8,128)(2,1)S(1)}, bf16[1536,256]{1,0:T(8,128)(2,1)S(1)}, bf16[256,256]{1,0:T(8,128)(2,1)S(1)}) custom-call(bf16[4,5,2,4,112,128]{5,4,3,2,1,0:T(8,128)(2,1)S(1)} %get-tuple-element.19.first_ref, bf16[4,3,80,128]{3,2,1,0:T(8,128)(2,1)S(1)} %get-tuple-element.15.west_ref, ...), custom_call_target="tpu_custom_call" | custom-call | flops 7000000000 | bytes 12582912 | tf_op jit(solution)/shard_map/inner_rows/pallas_call | solution.py:390
  28.8 0.0 collective-permute-done.2.p_ref
  28.8 0.0 collective-permute-done.3.q_ref
  28.8 7.8 %outer_rows.1 = bf16[4,48,112,128]{3,2,1,0:T(8,128)(2,1)} custom-call(bf16[4,5,80,128]{3,2,1,0:T(8,128)(2,1)S(1)} %get-tuple-element.17.p_own_ref, bf16[4,5,80,128]{3,2,1,0:T(8,128)(2,1)S(1)} %get-tuple-element.18.q_own_ref, bf16[4,5,80,128]{3,2,1,0:T(8,128)(2,1)S(1)} %collective-permute-done.2.p_ref, ...), custom_call_target="tpu_custom_call", output_to_operand_aliasing={{}: (8, {})} | custom-call | flops 5000000000 | bytes 6291456 | tf_op jit(solution)/shard_map/outer_rows/pallas_call | solution.py:455
  (1 shorter events, 0.0 us)
Async XLA Ops:
  0.0 2.1 %copy-start = (bf16[4,48,112,80]{2,3,1,0:T(8,128)(2,1)S(1)}, bf16[4,48,112,80]{2,3,1,0:T(8,128)(2,1)}, u32[]{:S(2)}) copy-start(bf16[4,48,112,80]{2,3,1,0:T(8,128)(2,1)} %param.5) | copy-start | bytes 10321924
  2.1 5.4 %copy-start.1 = (bf16[4,48,112,80]{2,3,1,0:T(8,128)(2,1)S(1)}, bf16[4,48,112,80]{2,3,1,0:T(8,128)(2,1)}, u32[]{:S(2)}) copy-start(bf16[4,48,112,80]{2,3,1,0:T(8,128)(2,1)} %param.5) | copy-start | bytes 10321924
  2.1 5.4 %copy-start.2 = (bf16[3,3,128,128]{3,2,1,0:T(8,128)(2,1)S(1)}, bf16[3,3,128,128]{3,2,1,0:T(8,128)(2,1)}, u32[]{:S(2)}) copy-start(bf16[3,3,128,128]{3,2,1,0:T(8,128)(2,1)} %near_ref.1) | copy-start | bytes 884740
  2.1 5.4 %copy-start.5 = (bf16[80,128]{1,0:T(8,128)(2,1)S(1)}, bf16[80,128]{1,0:T(8,128)(2,1)}, u32[]{:S(2)}) copy-start(bf16[80,128]{1,0:T(8,128)(2,1)} %lift_ref.1) | copy-start | bytes 61444
  4.2 9.7 %collective-permute-start = (bf16[4,3,80,128]{3,2,1,0:T(8,128)(2,1)S(1)}, bf16[4,3,80,128]{3,2,1,0:T(8,128)(2,1)S(1)}, u32[]{:S(2)}, u32[]{:S(2)}) collective-permute-start(bf16[4,3,80,128]{3,2,1,0:T(8,128)(2,1)S(1)} %get-tuple-element.15.west_ref), channel_id=1, source_target_pairs={{4,0},{8,4},{12,8},{16,12},{20,16},{24,20},{28,24},{0,28},{5,1},{9... | collective-permute-start | bytes 737288 | tf_op jit(solution)/shard_map/ppermute | solution.py:428
  7.5 7.4 %collective-permute-start.1 = (bf16[4,3,80,128]{3,2,1,0:T(8,128)(2,1)S(1)}, bf16[4,3,80,128]{3,2,1,0:T(8,128)(2,1)S(1)}, u32[]{:S(2)}, u32[]{:S(2)}) collective-permute-start(bf16[4,3,80,128]{3,2,1,0:T(8,128)(2,1)S(1)} %get-tuple-element.16.east_ref), channel_id=1, source_target_pairs={{28,0},{0,4},{4,8},{8,12},{12,16},{16,20},{20,24},{24,28},{29,1},{... | collective-permute-start | bytes 737288 | tf_op jit(solution)/shard_map/ppermute | solution.py:429
  13.8 5.0 %copy-start.3 = (bf16[3,3,128,128]{3,2,1,0:T(8,128)(2,1)S(1)}, bf16[3,3,128,128]{3,2,1,0:T(8,128)(2,1)}, u32[]{:S(2)}) copy-start(bf16[3,3,128,128]{3,2,1,0:T(8,128)(2,1)} %far_ref.1) | copy-start | bytes 884740
  13.9 5.0 %copy-start.4 = (bf16[128,128]{1,0:T(8,128)(2,1)S(1)}, bf16[128,128]{1,0:T(8,128)(2,1)}, u32[]{:S(2)}) copy-start(bf16[128,128]{1,0:T(8,128)(2,1)} %mix_ref.1) | copy-start | bytes 98308
  15.6 13.2 %collective-permute-start.2 = (bf16[4,5,80,128]{3,2,1,0:T(8,128)(2,1)S(1)}, bf16[4,5,80,128]{3,2,1,0:T(8,128)(2,1)S(1)}, u32[]{:S(2)}, u32[]{:S(2)}) collective-permute-start(bf16[4,5,80,128]{3,2,1,0:T(8,128)(2,1)S(1)} %get-tuple-element.17.p_own_ref), channel_id=1, source_target_pairs={{16,0},{20,4},{24,8},{28,12},{0,16},{4,20},{8,24},{12,28},{2,1},{6... | collective-permute-start | bytes 1228808 | tf_op jit(solution)/shard_map/ppermute | solution.py:449
  16.2 12.6 %collective-permute-start.3 = (bf16[4,5,80,128]{3,2,1,0:T(8,128)(2,1)S(1)}, bf16[4,5,80,128]{3,2,1,0:T(8,128)(2,1)S(1)}, u32[]{:S(2)}, u32[]{:S(2)}) collective-permute-start(bf16[4,5,80,128]{3,2,1,0:T(8,128)(2,1)S(1)} %get-tuple-element.18.q_own_ref), channel_id=1, source_target_pairs={{1,0},{5,4},{9,8},{13,12},{17,16},{21,20},{25,24},{29,28},{0,1},{4... | collective-permute-start | bytes 1228808 | tf_op jit(solution)/shard_map/ppermute | solution.py:450

commit v5 on v4

--- a/solution.py
+++ b/solution.py
@@ -13,12 +13,12 @@
 HALO = 5
 SLOT = 8
 WIDE = 1
-EVERY = 4
+EVERY = 2
 MIB = 1 << 20
 MADE = ((4, 256, 256), (6 * 256, 256), (256, 256))
 FIRST_MIB = 16
-INNER_MIB = 24
-OUTER_MIB = 34
+INNER_MIB = 20
+OUTER_MIB = 30
 PACK_MIB = 12
 
 
@@ -64,20 +64,36 @@
 
 
 def pack_columns(*refs):
-    *x_refs, west_ref, east_ref = refs
-    lane = lax.broadcasted_iota(jnp.int32, (west_ref.shape[2], 128), 1)
-    for group, x_ref in enumerate(x_refs):
-        cols = x_ref.shape[3]
-        rows = [widened(x_ref[0, i]) for i in range(x_ref.shape[1])]
-        moved = [turned(row, i * SLOT) for i, row in enumerate(rows)]
-        offset = cols - SLOT
-        west, east = moved[0], moved[0]
-        for i, row in enumerate(moved):
-            west = jnp.where(lane < i * SLOT, west, row)
-            at = (i * SLOT + offset) % 128
-            east = jnp.where((lane >= at) & (lane < at + SLOT), row, east)
-        west_ref[0, group] = west
-        east_ref[0, group] = turned(east, -offset)
+    *x_refs, west_ref, east_ref, choice = refs
+    per = 128 // SLOT
+    offset = x_refs[0].shape[3] - SLOT
+
+    @pl.when(pl.program_id(0) == 0)
+    def _():
+        source = lax.broadcasted_iota(jnp.int32, (128, 256), 0)
+        target = lax.broadcasted_iota(jnp.int32, (128, 256), 1)
+        is_east = target >= 128
+        lane = jnp.where(is_east, target - 128, target)
+        wanted = jnp.where(is_east, offset, 0) + lax.rem(lane, SLOT)
+        same = source == wanted
+        spot = lane // SLOT
+        for i in range(per):
+            keep = jnp.where(same & (spot == i), 1.0, 0.0)
+            choice[i * 128 : i * 128 + 128] = keep.astype(BF)
+
+    lhs = jnp.concatenate(
+        [
+            jnp.concatenate([widened(x_ref[0, i]) for i in range(per)], axis=1)
+            for x_ref in x_refs
+        ],
+        axis=0,
+    )
+    packed = dot(lhs, choice[...]).astype(BF)
+    cin = x_refs[0].shape[2]
+    for group in range(len(x_refs)):
+        rows = slice(group * cin, group * cin + cin)
+        west_ref[0, group] = packed[rows, :128]
+        east_ref[0, group] = packed[rows, 128:]
 
 
 def make_near(lift_ref, near_ref, wn_ref):
@@ -151,11 +167,14 @@
     return [v[base : base + height, 128 * o : 128 * o + 128] for o in range(2)]
 
 
-def first_rows(x_ref, lift_ref, near_ref, first_ref, wn_ref, *x3s):
+def first_rows(
+    x_ref, lift_ref, near_ref, far_ref, mix_ref, first_ref, wn_ref, wf_ref, wm_ref, *x3s
+):
 
     @pl.when(pl.program_id(0) == 0)
     def _():
         make_near(lift_ref, near_ref, wn_ref)
+        make_far(far_ref, mix_ref, wf_ref, wm_ref)
 
     cols = x_ref.shape[3]
     blocks = first_ref.shape[1]
@@ -191,7 +210,7 @@
     )
 
 
-def edge_strips(b, west_ref, east_ref, right_ref, left_ref, wn_ref, strips, pairs):
+def build_strips(b, west_ref, east_ref, right_ref, left_ref, strips):
     cin = west_ref.shape[2]
     per = 128 // SLOT
     lane = lax.rem(lax.broadcasted_iota(jnp.int32, (cin, 128), 1), SLOT)
@@ -201,27 +220,29 @@
         right, left = three_taps(right), three_taps(left)
         for i in range(per):
             at = slice(SLOT * i, SLOT * i + SLOT)
-            strips[b, per * g + i] = jnp.concatenate([right[at], left[at]], axis=0)
-    low = FAR - 1
-    rows = [[strips[b, low + 2 * q + i] for i in range(4)] for q in range(pairs)]
-    return near_block(rows, wn_ref)
+            strips[per * g + i] = jnp.concatenate([right[at], left[at]], axis=0)
 
 
 def inner_rows(
-    first_ref, west_ref, east_ref, right_ref, left_ref, wn_ref, far_ref, mix_ref,
-    out_ref, fx_ref, wf_ref, wm_ref, strips, edge, s, *f2s,
+    first_ref, west_ref, east_ref, right_ref, left_ref, wn_ref, wf_ref, wm_ref,
+    out_ref, fx_ref, edge, s, *scratch,
 ):
+    batch = west_ref.shape[0]
+    strips, f2s = scratch[:batch], scratch[batch:]
     blocks = len(f2s)
     cols = f2s[0].shape[-2] - 16
     pairs = 4 * blocks
 
     @pl.when(pl.program_id(0) == 0)
     def _():
-        make_far(far_ref, mix_ref, wf_ref, wm_ref)
-        for b in range(west_ref.shape[0]):
-            edge[b] = edge_strips(
-                b, west_ref, east_ref, right_ref, left_ref, wn_ref, strips, pairs
-            )
+        for b in range(batch + 1):
+            if b < batch:
+                build_strips(b, west_ref, east_ref, right_ref, left_ref, strips[b])
+            if b > 0:
+                rows = [
+                    [strips[b - 1][FAR - 1 + 2 * q + i] for i in range(4)] for q in range(pairs)
+                ]
+                edge[b - 1] = near_block(rows, wn_ref)
 
     sample = pl.program_id(0)
     span = 4 * cols
@@ -253,44 +274,53 @@
 
 def outer_rows(
     p_own_ref, q_own_ref, p_ref, q_ref, fx_ref,
-    wn_ref, wf_ref, wm_ref, _, out_ref, x3, f2, s, y, sems,
+    wn_ref, wf_ref, wm_ref, _, out_ref, s, y, sems, *scratch,
 ):
     lat = lax.axis_index("lat")
     even = lax.rem(lat, 2) == 0
     poles = (lat == 0, lat == lax.axis_size("lat") - 1)
-    cols = f2.shape[-2] - 16
+    units = [(b, side) for b in range(p_ref.shape[0]) for side in range(2)]
+    count = len(units)
+    x3s, f2s = scratch[:count], scratch[count:]
+    cols = f2s[0].shape[-2] - 16
     total = out_ref.shape[1]
     span = 4 * cols
-    units = [(b, side) for b in range(p_ref.shape[0]) for side in range(2)]
-    for u, (b, side) in enumerate(units):
+
+    def build(u):
+        b, side = units[u]
+        x3 = x3s[u]
         pole = poles[side]
         moved = pole if side == 0 else jnp.logical_not(pole)
         from_p = even if side == 0 else jnp.logical_not(even)
         base = jnp.where(moved, 1, 0)
         close = jnp.where(moved, 0, HALO - 1)
         for k in range(HALO):
-            taps = three_taps(jnp.where(from_p, p_ref[b, k], q_ref[b, k]))
-            x3[u, base + k] = taps
-        x3[u, 6 if side == 0 else 11] = x3[u, base + close]
+            x3[base + k] = three_taps(jnp.where(from_p, p_ref[b, k], q_ref[b, k]))
+        x3[6 if side == 0 else 11] = x3[base + close]
         for k in range(HALO):
             taps = three_taps(jnp.where(from_p, p_own_ref[b, k], q_own_ref[b, k]))
-            x3[u, (7 if side == 0 else 6) + k] = taps
+            x3[(7 if side == 0 else 6) + k] = taps
             if k == (0 if side == 0 else HALO - 1):
-                x3[u, jnp.where(moved, 0, HALO)] = taps
-    for u, (b, side) in enumerate(units):
+                x3[jnp.where(moved, 0, HALO)] = taps
+
+    def first(u):
+        b, side = units[u]
         pole = poles[side]
-        v = near_block(
-            [[x3[u, first + i] for i in range(4)] for first in (0, 2, 6, 8)], wn_ref
-        ).astype(BF)
+        rows = [[x3s[u][at + i] for i in range(4)] for at in (0, 2, 6, 8)]
+        v = near_block(rows, wn_ref).astype(BF)
         for q in range(2):
             for o, piece in enumerate(halves(v, q, 128)):
                 c = 2 * q + o
-                spread(f2, (u, side, jnp.where(pole, 3 - c, c)), side, piece)
+                spread(f2s[u], (side, jnp.where(pole, 3 - c, c)), side, piece)
             for o, piece in enumerate(halves(v, 2 + q, 128)):
-                spread(f2, (u, side, 2 * q + o), 1 - side, piece)
+                spread(f2s[u], (side, 2 * q + o), 1 - side, piece)
+
+    def known(u):
+        b, side = units[u]
         for h in range(2):
             for c in range(4):
-                spread(f2, (u, 1 - side, c), h, fx_ref[b, side, h, c])
+                spread(f2s[u], (1 - side, c), h, fx_ref[b, side, h, c])
+
     copies = []
 
     def finish(u):
@@ -304,8 +334,14 @@
         copy.start()
         copies.append(copy)
 
-    for u in range(len(units)):
-        s[u * span : (u + 1) * span] = far_block([(f2, (u, 0))], [(f2, (u, 1))], wf_ref)
+    build(0)
+    for u in range(count):
+        if u + 1 < count:
+            build(u + 1)
+        known(u)
+        first(u)
+    for u in range(count):
+        s[u * span : (u + 1) * span] = far_block([(f2s[u], (0,))], [(f2s[u], (1,))], wf_ref)
         if (u + 1) % EVERY == 0:
             for done_unit in range(u + 1 - EVERY, u + 1):
                 finish(done_unit)
@@ -360,6 +396,7 @@
         ],
         out_specs=[per_sample(edge)] * 2,
         out_shape=[jax.ShapeDtypeStruct(edge, BF)] * 2,
+        scratch_shapes=[pltpu.VMEM((128 * 128 // SLOT, 256), BF)],
         compiler_params=params(PACK_MIB),
         cost_estimate=cost(0, 4 * MIB),
         name="pack_columns",
@@ -373,17 +410,17 @@
     return pl.pallas_call(
         first_rows,
         grid=(batch,),
-        in_specs=[per_sample(x.shape)] + [whole(w.shape) for w in weights[:2]],
-        out_specs=[per_sample(first), whole(MADE[0])],
-        out_shape=[jax.ShapeDtypeStruct(shape, BF) for shape in (first, MADE[0])],
+        in_specs=[per_sample(x.shape)] + [whole(w.shape) for w in weights],
+        out_specs=[per_sample(first)] + [whole(shape) for shape in MADE],
+        out_shape=[jax.ShapeDtypeStruct(shape, BF) for shape in (first, *MADE)],
         scratch_shapes=[pltpu.VMEM((10, cols, 256), BF)] * (rows // 8 - 1),
         compiler_params=params(FIRST_MIB),
         cost_estimate=cost(6 * 10**9, 9 * MIB),
         name="first_rows",
-    )(x, *weights[:2])
-
-
-def call_inner(first, wn, west, east, right, left, weights, rows):
+    )(x, *weights)
+
+
+def call_inner(first, west, east, right, left, made, rows):
     batch, blocks, _, _, cols, chan = first.shape
     fx = (batch, 2, 2, 4, 128, chan)
     inner = rows - 16
@@ -392,30 +429,28 @@
         grid=(batch,),
         in_specs=[per_sample(first.shape)]
         + [whole(right.shape)] * 4
-        + [whole(w.shape) for w in (wn, *weights[2:])],
+        + [whole(shape) for shape in MADE],
         out_specs=[
             pl.BlockSpec(
                 (pl.Element(1), pl.Element(inner), pl.Element(cols), pl.Element(chan)),
                 lambda b: (b, 8, 0, 0),
             ),
             per_sample(fx),
-            whole(MADE[1]),
-            whole(MADE[2]),
         ],
         out_shape=[
             jax.ShapeDtypeStruct(shape, BF)
-            for shape in ((batch, rows, cols, chan), fx, MADE[1], MADE[2])
+            for shape in ((batch, rows, cols, chan), fx)
         ],
         scratch_shapes=[
-            pltpu.VMEM((batch, rows, 16, 256), BF),
             pltpu.VMEM((batch, 16 * 4 * blocks, 256), F32),
             pltpu.VMEM(((blocks - 1) * 4 * cols, 256), BF),
         ]
+        + [pltpu.VMEM((rows, 16, 256), BF)] * batch
         + [pltpu.VMEM((4, cols + 16, 256), BF)] * blocks,
         compiler_params=params(INNER_MIB),
         cost_estimate=cost(7 * 10**9, 12 * MIB),
         name="inner_rows",
-    )(first, west, east, right, left, wn, *weights[2:])
+    )(first, west, east, right, left, *made)
 
 
 def on_device(fields, lift_weight, near_kernel, far_kernel, mix_weight):
@@ -428,7 +463,7 @@
     right = lax.ppermute(west, "lon", [((i + 1) % lons, i) for i in range(lons)])
     left = lax.ppermute(east, "lon", [((i - 1) % lons, i) for i in range(lons)])
     weights = (lift_weight, near_kernel, far_kernel, mix_weight)
-    first, wn = call_first(x, weights)
+    first, *made = call_first(x, weights)
     strip = (batch, HALO, cin, 128)
     last = rows // 8 - 1
     p_send, q_send = pl.pallas_call(
@@ -449,7 +484,7 @@
     p_got = lax.ppermute(p_send, ("lon", "lat"), swaps(lats, lons, 1))
     q_got = lax.ppermute(q_send, ("lon", "lat"), swaps(lats, lons, 0))
 
-    out, edges, wf, wm = call_inner(first, wn, west, east, right, left, weights, rows)
+    out, edges = call_inner(first, west, east, right, left, made, rows)
     units = 2 * batch
     fx = edges.shape
     return pl.pallas_call(
@@ -462,17 +497,17 @@
         out_specs=pl.BlockSpec(memory_space=pl.ANY),
         out_shape=jax.ShapeDtypeStruct((batch, rows, cols, chan), BF),
         scratch_shapes=[
-            pltpu.VMEM((units, 12, 128, 256), BF),
-            pltpu.VMEM((units, 2, 4, cols + 16, 256), BF),
             pltpu.VMEM((units * 4 * cols, 256), BF),
             pltpu.VMEM((units, 8, cols, chan), BF),
             pltpu.SemaphoreType.DMA((units,)),
-        ],
+        ]
+        + [pltpu.VMEM((12, 128, 256), BF)] * units
+        + [pltpu.VMEM((2, 4, cols + 16, 256), BF)] * units,
         input_output_aliases={8: 0},
         compiler_params=params(OUTER_MIB),
         cost_estimate=cost(5 * 10**9, 6 * MIB),
         name="outer_rows",
-    )(p_send, q_send, p_got, q_got, edges, wn, wf, wm, out)
+    )(p_send, q_send, p_got, q_got, edges, *made, out)
 
 
 def solution(mesh):

time: 36.8 us -> 36.3 us (0.986)
  Pallas kernels: 26.8 us -> 26.3 us
  transfers between devices with their start and end apart: 4 -> 4, of which waited for: 1 -> 1; matrix products, arithmetic and copies ran while one was open for 0% -> 0% of each run, Pallas kernels for 44% -> 45%
where the time goes in v5:
time: 36.3 us; the launch traced here: 36.2 us
  Pallas kernels  26.3 us (72%)
  starting transfers between devices  6.61 us (18%)
  local copies, waits for them, and re-layouts  2.13 us (6%)
  waiting for transfers between devices  1.01 us (3%)
    pallas_call x1, Pallas kernels, call_inner(): pl.pallas_call(inner_rows, grid=(batch,), in_specs=[per_sample(first.shap...  9.96 us
    pallas_call x1, Pallas kernels, on_device(): pl.pallas_call(outer_rows, grid=(1,), in_specs=[whole(strip)] * 4 + [whol...  7.52 us
    pallas_call x1, Pallas kernels, call_first(): pl.pallas_call(first_rows, grid=(batch,), in_specs=[per_sample(x.shape)]...  6.31 us
    ppermute x1, starting transfers between devices, on_device(): lax.ppermute(west, 'lon', [((i + 1) % lons, i) for i in range(lons)])  3.39 us
    ppermute x1, starting transfers between devices, on_device(): q_got = lax.ppermute(q_send, ('lon', 'lat'), swaps(lats, lons, 0))  2.65 us
    unnamed x12, local copies, waits for them, and re-layouts  2.13 us
    pallas_call x1, Pallas kernels, call_pack(): pl.pallas_call(pack_columns, grid=(x.shape[0],), in_specs=[pl.BlockSpec((...  1.84 us
    ppermute x1, waiting for transfers between devices, on_device(): left = lax.ppermute(east, 'lon', [((i - 1) % lons, i) for i in range(lons)])  1 us
  transfers between devices with their start and end apart: 4, of which 1 were waited for; matrix products, arithmetic and copies ran while one was open for 0% of the time, Pallas kernels for 45%

profile of v5, /device:TPU:0, one launch (start us, length us, event | category | flops | bytes accessed | tf_op | source)
XLA Modules:
  0.0 36.2 jit_solution(8879185227782872891)
XLA Ops:
  0.0 0.0 copy-start
  0.0 2.1 %copy-done = bf16[4,48,112,80]{2,3,1,0:T(8,128)(2,1)S(1)} copy-done((bf16[4,48,112,80]{2,3,1,0:T(8,128)(2,1)S(1)}, bf16[4,48,112,80]{2,3,1,0:T(8,128)(2,1)}, u32[]{:S(2)}) %copy-start) | copy-done | bytes 3440664
  2.1 0.0 copy-start.1
  2.1 0.0 copy-start.2
  2.1 0.0 copy-start.3
  2.1 0.0 copy-start.5
  2.1 1.8 %pack_columns.1 = (bf16[4,3,80,128]{3,2,1,0:T(8,128)(2,1)S(1)}, bf16[4,3,80,128]{3,2,1,0:T(8,128)(2,1)S(1)}) custom-call(bf16[4,48,80,112]{3,2,1,0:T(8,128)(2,1)S(1)} %bitcast.1, bf16[4,48,80,112]{3,2,1,0:T(8,128)(2,1)S(1)} %bitcast.2, bf16[4,48,80,112]{3,2,1,0:T(8,128)(2,1)S(1)} %bitcast.3), custom_call_target="tpu_custom_call" | custom-call | bytes 4194304 | tf_op jit(solution)/shard_map/pack_columns/pallas_call | solution.py:388
  4.0 3.4 %collective-permute-start = (bf16[4,3,80,128]{3,2,1,0:T(8,128)(2,1)S(1)}, bf16[4,3,80,128]{3,2,1,0:T(8,128)(2,1)S(1)}, u32[]{:S(2)}, u32[]{:S(2)}) collective-permute-start(bf16[4,3,80,128]{3,2,1,0:T(8,128)(2,1)S(1)} %get-tuple-element.15.west_ref), channel_id=1, source_target_pairs={{4,0},{8,4},{12,8},{16,12},{20,16},{24,20},{28,24},{0,28},{5,1},{9... | collective-permute-start | bytes 737288 | tf_op jit(solution)/shard_map/ppermute | solution.py:463
  7.4 0.0 collective-permute-start.1
  7.4 0.0 copy-done.1
  7.4 0.0 copy-done.2
  7.4 0.0 copy-done.3
  7.4 0.0 copy-done.4
  7.4 0.0 copy-done.5
  7.4 6.3 %first_rows.1 = (bf16[4,5,2,4,112,128]{5,4,3,2,1,0:T(8,128)(2,1)S(1)}, bf16[4,256,256]{2,1,0:T(8,128)(2,1)S(1)}, bf16[1536,256]{1,0:T(8,128)(2,1)S(1)}, bf16[256,256]{1,0:T(8,128)(2,1)S(1)}) custom-call(bf16[4,48,80,112]{3,2,1,0:T(8,128)(2,1)S(1)} %bitcast.4, bf16[80,128]{1,0:T(8,128)(2,1)S(1)} %copy-done.5, bf16[3,3,128,128]{3,2,1,0:T(8,128)(2,1)S(1)} %copy-done.2, ...), custom_call_target="tpu_custom_call" | custom-call | flops 6000000000 | bytes 9437184 | tf_op jit(solution)/shard_map/first_rows/pallas_call | solution.py:410
  13.7 0.0 collective-permute-done.right_ref
  13.7 1.0 %collective-permute-done.1.left_ref = bf16[4,3,80,128]{3,2,1,0:T(8,128)(2,1)S(1)} collective-permute-done((bf16[4,3,80,128]{3,2,1,0:T(8,128)(2,1)S(1)}, bf16[4,3,80,128]{3,2,1,0:T(8,128)(2,1)S(1)}, u32[]{:S(2)}, u32[]{:S(2)}) %collective-permute-start.1) | collective-permute-done | bytes 245792 | tf_op jit(solution)/shard_map/ppermute | solution.py:464
  14.7 0.7 %pack_rows.1 = (bf16[4,5,80,128]{3,2,1,0:T(8,128)(2,1)S(1)}, bf16[4,5,80,128]{3,2,1,0:T(8,128)(2,1)S(1)}) custom-call(bf16[4,48,80,112]{3,2,1,0:T(8,128)(2,1)S(1)} %bitcast.5, bf16[4,48,80,112]{3,2,1,0:T(8,128)(2,1)S(1)} %bitcast.6, bf16[4,3,80,128]{3,2,1,0:T(8,128)(2,1)S(1)} %collective-permute-done.right_ref, ...), custom_call_target="tpu_custom_call" | custom-call | bytes 2097152 | tf_op jit(solution)/shard_map/pack_rows/pallas_call | solution.py:469
  15.5 0.6 %collective-permute-start.2 = (bf16[4,5,80,128]{3,2,1,0:T(8,128)(2,1)S(1)}, bf16[4,5,80,128]{3,2,1,0:T(8,128)(2,1)S(1)}, u32[]{:S(2)}, u32[]{:S(2)}) collective-permute-start(bf16[4,5,80,128]{3,2,1,0:T(8,128)(2,1)S(1)} %get-tuple-element.17.p_own_ref), channel_id=1, source_target_pairs={{16,0},{20,4},{24,8},{28,12},{0,16},{4,20},{8,24},{12,28},{2,1},{6... | collective-permute-start | bytes 1228808 | tf_op jit(solution)/shard_map/ppermute | solution.py:484
  16.0 2.6 %collective-permute-start.3 = (bf16[4,5,80,128]{3,2,1,0:T(8,128)(2,1)S(1)}, bf16[4,5,80,128]{3,2,1,0:T(8,128)(2,1)S(1)}, u32[]{:S(2)}, u32[]{:S(2)}) collective-permute-start(bf16[4,5,80,128]{3,2,1,0:T(8,128)(2,1)S(1)} %get-tuple-element.18.q_own_ref), channel_id=1, source_target_pairs={{1,0},{5,4},{9,8},{13,12},{17,16},{21,20},{25,24},{29,28},{0,1},{4... | collective-permute-start | bytes 1228808 | tf_op jit(solution)/shard_map/ppermute | solution.py:485
  18.7 10.0 %inner_rows.1 = (bf16[4,48,112,128]{3,2,1,0:T(8,128)(2,1)}, bf16[4,2,2,4,128,128]{5,4,3,2,1,0:T(8,128)(2,1)S(1)}) custom-call(bf16[4,5,2,4,112,128]{5,4,3,2,1,0:T(8,128)(2,1)S(1)} %get-tuple-element.19.first_ref, bf16[4,3,80,128]{3,2,1,0:T(8,128)(2,1)S(1)} %get-tuple-element.15.west_ref, bf16[4,3,80,128]{3,2,1,0:T(8,128)(2,1)S(1)} %get-tuple-element.16.east_ref, ...), custom_call_target="tpu_custom_call" | custom-call | flops 7000000000 | bytes 12582912 | tf_op jit(solution)/shard_map/inner_rows/pallas_call | solution.py:427
  28.6 0.0 collective-permute-done.2.p_ref
  28.6 0.0 collective-permute-done.3.q_ref
  28.6 7.5 %outer_rows.1 = bf16[4,48,112,128]{3,2,1,0:T(8,128)(2,1)} custom-call(bf16[4,5,80,128]{3,2,1,0:T(8,128)(2,1)S(1)} %get-tuple-element.17.p_own_ref, bf16[4,5,80,128]{3,2,1,0:T(8,128)(2,1)S(1)} %get-tuple-element.18.q_own_ref, bf16[4,5,80,128]{3,2,1,0:T(8,128)(2,1)S(1)} %collective-permute-done.2.p_ref, ...), custom_call_target="tpu_custom_call", output_to_operand_aliasing={{}: (8, {})} | custom-call | flops 5000000000 | bytes 6291456 | tf_op jit(solution)/shard_map/outer_rows/pallas_call | solution.py:490
  (1 shorter events, 0.0 us)
Async XLA Ops:
  0.0 2.1 %copy-start = (bf16[4,48,112,80]{2,3,1,0:T(8,128)(2,1)S(1)}, bf16[4,48,112,80]{2,3,1,0:T(8,128)(2,1)}, u32[]{:S(2)}) copy-start(bf16[4,48,112,80]{2,3,1,0:T(8,128)(2,1)} %param.5) | copy-start | bytes 10321924
  2.1 5.3 %copy-start.1 = (bf16[4,48,112,80]{2,3,1,0:T(8,128)(2,1)S(1)}, bf16[4,48,112,80]{2,3,1,0:T(8,128)(2,1)}, u32[]{:S(2)}) copy-start(bf16[4,48,112,80]{2,3,1,0:T(8,128)(2,1)} %param.5) | copy-start | bytes 10321924
  2.1 5.3 %copy-start.2 = (bf16[3,3,128,128]{3,2,1,0:T(8,128)(2,1)S(1)}, bf16[3,3,128,128]{3,2,1,0:T(8,128)(2,1)}, u32[]{:S(2)}) copy-start(bf16[3,3,128,128]{3,2,1,0:T(8,128)(2,1)} %near_ref.1) | copy-start | bytes 884740
  2.1 5.3 %copy-start.3 = (bf16[3,3,128,128]{3,2,1,0:T(8,128)(2,1)S(1)}, bf16[3,3,128,128]{3,2,1,0:T(8,128)(2,1)}, u32[]{:S(2)}) copy-start(bf16[3,3,128,128]{3,2,1,0:T(8,128)(2,1)} %far_ref.1) | copy-start | bytes 884740
  2.1 5.3 %copy-start.4 = (bf16[128,128]{1,0:T(8,128)(2,1)S(1)}, bf16[128,128]{1,0:T(8,128)(2,1)}, u32[]{:S(2)}) copy-start(bf16[128,128]{1,0:T(8,128)(2,1)} %mix_ref.1) | copy-start | bytes 98308
  2.1 5.3 %copy-start.5 = (bf16[80,128]{1,0:T(8,128)(2,1)S(1)}, bf16[80,128]{1,0:T(8,128)(2,1)}, u32[]{:S(2)}) copy-start(bf16[80,128]{1,0:T(8,128)(2,1)} %lift_ref.1) | copy-start | bytes 61444
  4.0 9.7 %collective-permute-start = (bf16[4,3,80,128]{3,2,1,0:T(8,128)(2,1)S(1)}, bf16[4,3,80,128]{3,2,1,0:T(8,128)(2,1)S(1)}, u32[]{:S(2)}, u32[]{:S(2)}) collective-permute-start(bf16[4,3,80,128]{3,2,1,0:T(8,128)(2,1)S(1)} %get-tuple-element.15.west_ref), channel_id=1, source_target_pairs={{4,0},{8,4},{12,8},{16,12},{20,16},{24,20},{28,24},{0,28},{5,1},{9... | collective-permute-start | bytes 737288 | tf_op jit(solution)/shard_map/ppermute | solution.py:463
  7.4 7.4 %collective-permute-start.1 = (bf16[4,3,80,128]{3,2,1,0:T(8,128)(2,1)S(1)}, bf16[4,3,80,128]{3,2,1,0:T(8,128)(2,1)S(1)}, u32[]{:S(2)}, u32[]{:S(2)}) collective-permute-start(bf16[4,3,80,128]{3,2,1,0:T(8,128)(2,1)S(1)} %get-tuple-element.16.east_ref), channel_id=1, source_target_pairs={{28,0},{0,4},{4,8},{8,12},{12,16},{16,20},{20,24},{24,28},{29,1},{... | collective-permute-start | bytes 737288 | tf_op jit(solution)/shard_map/ppermute | solution.py:464
  15.5 13.2 %collective-permute-start.2 = (bf16[4,5,80,128]{3,2,1,0:T(8,128)(2,1)S(1)}, bf16[4,5,80,128]{3,2,1,0:T(8,128)(2,1)S(1)}, u32[]{:S(2)}, u32[]{:S(2)}) collective-permute-start(bf16[4,5,80,128]{3,2,1,0:T(8,128)(2,1)S(1)} %get-tuple-element.17.p_own_ref), channel_id=1, source_target_pairs={{16,0},{20,4},{24,8},{28,12},{0,16},{4,20},{8,24},{12,28},{2,1},{6... | collective-permute-start | bytes 1228808 | tf_op jit(solution)/shard_map/ppermute | solution.py:484
  16.0 12.6 %collective-permute-start.3 = (bf16[4,5,80,128]{3,2,1,0:T(8,128)(2,1)S(1)}, bf16[4,5,80,128]{3,2,1,0:T(8,128)(2,1)S(1)}, u32[]{:S(2)}, u32[]{:S(2)}) collective-permute-start(bf16[4,5,80,128]{3,2,1,0:T(8,128)(2,1)S(1)} %get-tuple-element.18.q_own_ref), channel_id=1, source_target_pairs={{1,0},{5,4},{9,8},{13,12},{17,16},{21,20},{25,24},{29,28},{0,1},{4... | collective-permute-start | bytes 1228808 | tf_op jit(solution)/shard_map/ppermute | solution.py:485

commit v6 on v5

--- a/solution.py
+++ b/solution.py
@@ -133,9 +133,12 @@
         q_ref[0, k] = jnp.where(even, bottom[k], top[k])
 
 
-def spread(f2, at, half, piece):
-    turned_piece = jnp.concatenate([piece[128 - FAR :], piece[: 128 - FAR]], axis=0)
-    f2[(*at, slice(None), slice(half * 128, half * 128 + 128))] = turned_piece
+def past_edges(piece):
+    return jnp.concatenate([piece[128 - FAR :], piece[: 128 - FAR]], axis=0)
+
+
+def place(f2, at, half, piece):
+    f2[(*at, slice(None), slice(half * 128, half * 128 + 128))] = piece
 
 
 def tap(ref, b, at, c):
@@ -256,8 +259,8 @@
             q = 4 * m + p
             for o, strip in enumerate(halves(edge[sample, 16 * q : 16 * q + 16], 0, 16)):
                 h, c = divmod(2 * p + o, 4)
-                piece = joined(first_ref[0, m, h, c], strip)
-                spread(f2s[m], (c,), h, piece)
+                piece = past_edges(joined(first_ref[0, m, h, c], strip))
+                place(f2s[m], (c,), h, piece)
                 if m == 0:
                     fx_ref[0, 0, h, c] = piece
                 if m == blocks - 1:
@@ -311,15 +314,16 @@
         for q in range(2):
             for o, piece in enumerate(halves(v, q, 128)):
                 c = 2 * q + o
-                spread(f2s[u], (side, jnp.where(pole, 3 - c, c)), side, piece)
+                row = jnp.where(pole, 3 - c, c)
+                place(f2s[u], (side, row), side, past_edges(piece))
             for o, piece in enumerate(halves(v, 2 + q, 128)):
-                spread(f2s[u], (side, 2 * q + o), 1 - side, piece)
+                place(f2s[u], (side, 2 * q + o), 1 - side, past_edges(piece))
 
     def known(u):
         b, side = units[u]
         for h in range(2):
             for c in range(4):
-                spread(f2s[u], (1 - side, c), h, fx_ref[b, side, h, c])
+                place(f2s[u], (1 - side, c), h, fx_ref[b, side, h, c])
 
     copies = []
 

time: 36.3 us -> 36.3 us (level)
  no operation moved by 1% of the time
where the time goes in v6:
time: 36.3 us; the launch traced here: 36.2 us
  Pallas kernels  26.3 us (72%)
  starting transfers between devices  6.61 us (18%)
  local copies, waits for them, and re-layouts  2.13 us (6%)
  waiting for transfers between devices  1.01 us (3%)
    pallas_call x1, Pallas kernels, call_inner(): pl.pallas_call(inner_rows, grid=(batch,), in_specs=[per_sample(first.shap...  9.99 us
    pallas_call x1, Pallas kernels, on_device(): pl.pallas_call(outer_rows, grid=(1,), in_specs=[whole(strip)] * 4 + [whol...  7.48 us
    pallas_call x1, Pallas kernels, call_first(): pl.pallas_call(first_rows, grid=(batch,), in_specs=[per_sample(x.shape)]...  6.31 us
    ppermute x1, starting transfers between devices, on_device(): lax.ppermute(west, 'lon', [((i + 1) % lons, i) for i in range(lons)])  3.39 us
    ppermute x1, starting transfers between devices, on_device(): q_got = lax.ppermute(q_send, ('lon', 'lat'), swaps(lats, lons, 0))  2.65 us
    unnamed x12, local copies, waits for them, and re-layouts  2.13 us
    pallas_call x1, Pallas kernels, call_pack(): pl.pallas_call(pack_columns, grid=(x.shape[0],), in_specs=[pl.BlockSpec((...  1.84 us
    ppermute x1, waiting for transfers between devices, on_device(): left = lax.ppermute(east, 'lon', [((i - 1) % lons, i) for i in range(lons)])  1 us
  transfers between devices with their start and end apart: 4, of which 1 were waited for; matrix products, arithmetic and copies ran while one was open for 0% of the time, Pallas kernels for 45%

profile of v6, /device:TPU:0, one launch (start us, length us, event | category | flops | bytes accessed | tf_op | source)
XLA Modules:
  0.0 36.2 jit_solution(3611930031755979494)
XLA Ops:
  0.0 0.0 copy-start
  0.0 2.1 %copy-done = bf16[4,48,112,80]{2,3,1,0:T(8,128)(2,1)S(1)} copy-done((bf16[4,48,112,80]{2,3,1,0:T(8,128)(2,1)S(1)}, bf16[4,48,112,80]{2,3,1,0:T(8,128)(2,1)}, u32[]{:S(2)}) %copy-start) | copy-done | bytes 3440664
  2.1 0.0 copy-start.2
  2.1 0.0 copy-start.3
  2.1 0.0 copy-start.4
  2.1 0.0 copy-start.5
  2.1 1.8 %pack_columns.1 = (bf16[4,3,80,128]{3,2,1,0:T(8,128)(2,1)S(1)}, bf16[4,3,80,128]{3,2,1,0:T(8,128)(2,1)S(1)}) custom-call(bf16[4,48,80,112]{3,2,1,0:T(8,128)(2,1)S(1)} %bitcast.1, bf16[4,48,80,112]{3,2,1,0:T(8,128)(2,1)S(1)} %bitcast.2, bf16[4,48,80,112]{3,2,1,0:T(8,128)(2,1)S(1)} %bitcast.3), custom_call_target="tpu_custom_call" | custom-call | bytes 4194304 | tf_op jit(solution)/shard_map/pack_columns/pallas_call | solution.py:392
  4.0 3.4 %collective-permute-start = (bf16[4,3,80,128]{3,2,1,0:T(8,128)(2,1)S(1)}, bf16[4,3,80,128]{3,2,1,0:T(8,128)(2,1)S(1)}, u32[]{:S(2)}, u32[]{:S(2)}) collective-permute-start(bf16[4,3,80,128]{3,2,1,0:T(8,128)(2,1)S(1)} %get-tuple-element.15.west_ref), channel_id=1, source_target_pairs={{4,0},{8,4},{12,8},{16,12},{20,16},{24,20},{28,24},{0,28},{5,1},{9... | collective-permute-start | bytes 737288 | tf_op jit(solution)/shard_map/ppermute | solution.py:467
  7.4 0.0 collective-permute-start.1
  7.4 0.0 copy-done.1
  7.4 0.0 copy-done.2
  7.4 0.0 copy-done.3
  7.4 0.0 copy-done.4
  7.4 0.0 copy-done.5
  7.4 6.3 %first_rows.1 = (bf16[4,5,2,4,112,128]{5,4,3,2,1,0:T(8,128)(2,1)S(1)}, bf16[4,256,256]{2,1,0:T(8,128)(2,1)S(1)}, bf16[1536,256]{1,0:T(8,128)(2,1)S(1)}, bf16[256,256]{1,0:T(8,128)(2,1)S(1)}) custom-call(bf16[4,48,80,112]{3,2,1,0:T(8,128)(2,1)S(1)} %bitcast.4, bf16[80,128]{1,0:T(8,128)(2,1)S(1)} %copy-done.5, bf16[3,3,128,128]{3,2,1,0:T(8,128)(2,1)S(1)} %copy-done.2, ...), custom_call_target="tpu_custom_call" | custom-call | flops 6000000000 | bytes 9437184 | tf_op jit(solution)/shard_map/first_rows/pallas_call | solution.py:414
  13.7 0.0 collective-permute-done.right_ref
  13.7 1.0 %collective-permute-done.1.left_ref = bf16[4,3,80,128]{3,2,1,0:T(8,128)(2,1)S(1)} collective-permute-done((bf16[4,3,80,128]{3,2,1,0:T(8,128)(2,1)S(1)}, bf16[4,3,80,128]{3,2,1,0:T(8,128)(2,1)S(1)}, u32[]{:S(2)}, u32[]{:S(2)}) %collective-permute-start.1) | collective-permute-done | bytes 245792 | tf_op jit(solution)/shard_map/ppermute | solution.py:468
  14.7 0.7 %pack_rows.1 = (bf16[4,5,80,128]{3,2,1,0:T(8,128)(2,1)S(1)}, bf16[4,5,80,128]{3,2,1,0:T(8,128)(2,1)S(1)}) custom-call(bf16[4,48,80,112]{3,2,1,0:T(8,128)(2,1)S(1)} %bitcast.5, bf16[4,48,80,112]{3,2,1,0:T(8,128)(2,1)S(1)} %bitcast.6, bf16[4,3,80,128]{3,2,1,0:T(8,128)(2,1)S(1)} %collective-permute-done.right_ref, ...), custom_call_target="tpu_custom_call" | custom-call | bytes 2097152 | tf_op jit(solution)/shard_map/pack_rows/pallas_call | solution.py:473
  15.5 0.6 %collective-permute-start.2 = (bf16[4,5,80,128]{3,2,1,0:T(8,128)(2,1)S(1)}, bf16[4,5,80,128]{3,2,1,0:T(8,128)(2,1)S(1)}, u32[]{:S(2)}, u32[]{:S(2)}) collective-permute-start(bf16[4,5,80,128]{3,2,1,0:T(8,128)(2,1)S(1)} %get-tuple-element.17.p_own_ref), channel_id=1, source_target_pairs={{16,0},{20,4},{24,8},{28,12},{0,16},{4,20},{8,24},{12,28},{2,1},{6... | collective-permute-start | bytes 1228808 | tf_op jit(solution)/shard_map/ppermute | solution.py:488
  16.0 2.6 %collective-permute-start.3 = (bf16[4,5,80,128]{3,2,1,0:T(8,128)(2,1)S(1)}, bf16[4,5,80,128]{3,2,1,0:T(8,128)(2,1)S(1)}, u32[]{:S(2)}, u32[]{:S(2)}) collective-permute-start(bf16[4,5,80,128]{3,2,1,0:T(8,128)(2,1)S(1)} %get-tuple-element.18.q_own_ref), channel_id=1, source_target_pairs={{1,0},{5,4},{9,8},{13,12},{17,16},{21,20},{25,24},{29,28},{0,1},{4... | collective-permute-start | bytes 1228808 | tf_op jit(solution)/shard_map/ppermute | solution.py:489
  18.7 10.0 %inner_rows.1 = (bf16[4,48,112,128]{3,2,1,0:T(8,128)(2,1)}, bf16[4,2,2,4,128,128]{5,4,3,2,1,0:T(8,128)(2,1)S(1)}) custom-call(bf16[4,5,2,4,112,128]{5,4,3,2,1,0:T(8,128)(2,1)S(1)} %get-tuple-element.19.first_ref, bf16[4,3,80,128]{3,2,1,0:T(8,128)(2,1)S(1)} %get-tuple-element.15.west_ref, bf16[4,3,80,128]{3,2,1,0:T(8,128)(2,1)S(1)} %get-tuple-element.16.east_ref, ...), custom_call_target="tpu_custom_call" | custom-call | flops 7000000000 | bytes 12582912 | tf_op jit(solution)/shard_map/inner_rows/pallas_call | solution.py:431
  28.7 0.0 collective-permute-done.2.p_ref
  28.7 0.0 collective-permute-done.3.q_ref
  28.7 7.5 %outer_rows.1 = bf16[4,48,112,128]{3,2,1,0:T(8,128)(2,1)} custom-call(bf16[4,5,80,128]{3,2,1,0:T(8,128)(2,1)S(1)} %get-tuple-element.17.p_own_ref, bf16[4,5,80,128]{3,2,1,0:T(8,128)(2,1)S(1)} %get-tuple-element.18.q_own_ref, bf16[4,5,80,128]{3,2,1,0:T(8,128)(2,1)S(1)} %collective-permute-done.2.p_ref, ...), custom_call_target="tpu_custom_call", output_to_operand_aliasing={{}: (8, {})} | custom-call | flops 5000000000 | bytes 6291456 | tf_op jit(solution)/shard_map/outer_rows/pallas_call | solution.py:494
  (1 shorter events, 0.0 us)
Async XLA Ops:
  0.0 2.1 %copy-start = (bf16[4,48,112,80]{2,3,1,0:T(8,128)(2,1)S(1)}, bf16[4,48,112,80]{2,3,1,0:T(8,128)(2,1)}, u32[]{:S(2)}) copy-start(bf16[4,48,112,80]{2,3,1,0:T(8,128)(2,1)} %param.5) | copy-start | bytes 10321924
  2.1 5.3 %copy-start.1 = (bf16[4,48,112,80]{2,3,1,0:T(8,128)(2,1)S(1)}, bf16[4,48,112,80]{2,3,1,0:T(8,128)(2,1)}, u32[]{:S(2)}) copy-start(bf16[4,48,112,80]{2,3,1,0:T(8,128)(2,1)} %param.5) | copy-start | bytes 10321924
  2.1 5.3 %copy-start.2 = (bf16[3,3,128,128]{3,2,1,0:T(8,128)(2,1)S(1)}, bf16[3,3,128,128]{3,2,1,0:T(8,128)(2,1)}, u32[]{:S(2)}) copy-start(bf16[3,3,128,128]{3,2,1,0:T(8,128)(2,1)} %near_ref.1) | copy-start | bytes 884740
  2.1 5.3 %copy-start.3 = (bf16[3,3,128,128]{3,2,1,0:T(8,128)(2,1)S(1)}, bf16[3,3,128,128]{3,2,1,0:T(8,128)(2,1)}, u32[]{:S(2)}) copy-start(bf16[3,3,128,128]{3,2,1,0:T(8,128)(2,1)} %far_ref.1) | copy-start | bytes 884740
  2.1 5.3 %copy-start.4 = (bf16[128,128]{1,0:T(8,128)(2,1)S(1)}, bf16[128,128]{1,0:T(8,128)(2,1)}, u32[]{:S(2)}) copy-start(bf16[128,128]{1,0:T(8,128)(2,1)} %mix_ref.1) | copy-start | bytes 98308
  2.1 5.3 %copy-start.5 = (bf16[80,128]{1,0:T(8,128)(2,1)S(1)}, bf16[80,128]{1,0:T(8,128)(2,1)}, u32[]{:S(2)}) copy-start(bf16[80,128]{1,0:T(8,128)(2,1)} %lift_ref.1) | copy-start | bytes 61444
  4.0 9.7 %collective-permute-start = (bf16[4,3,80,128]{3,2,1,0:T(8,128)(2,1)S(1)}, bf16[4,3,80,128]{3,2,1,0:T(8,128)(2,1)S(1)}, u32[]{:S(2)}, u32[]{:S(2)}) collective-permute-start(bf16[4,3,80,128]{3,2,1,0:T(8,128)(2,1)S(1)} %get-tuple-element.15.west_ref), channel_id=1, source_target_pairs={{4,0},{8,4},{12,8},{16,12},{20,16},{24,20},{28,24},{0,28},{5,1},{9... | collective-permute-start | bytes 737288 | tf_op jit(solution)/shard_map/ppermute | solution.py:467
  7.4 7.4 %collective-permute-start.1 = (bf16[4,3,80,128]{3,2,1,0:T(8,128)(2,1)S(1)}, bf16[4,3,80,128]{3,2,1,0:T(8,128)(2,1)S(1)}, u32[]{:S(2)}, u32[]{:S(2)}) collective-permute-start(bf16[4,3,80,128]{3,2,1,0:T(8,128)(2,1)S(1)} %get-tuple-element.16.east_ref), channel_id=1, source_target_pairs={{28,0},{0,4},{4,8},{8,12},{12,16},{16,20},{20,24},{24,28},{29,1},{... | collective-permute-start | bytes 737288 | tf_op jit(solution)/shard_map/ppermute | solution.py:468
  15.5 13.2 %collective-permute-start.2 = (bf16[4,5,80,128]{3,2,1,0:T(8,128)(2,1)S(1)}, bf16[4,5,80,128]{3,2,1,0:T(8,128)(2,1)S(1)}, u32[]{:S(2)}, u32[]{:S(2)}) collective-permute-start(bf16[4,5,80,128]{3,2,1,0:T(8,128)(2,1)S(1)} %get-tuple-element.17.p_own_ref), channel_id=1, source_target_pairs={{16,0},{20,4},{24,8},{28,12},{0,16},{4,20},{8,24},{12,28},{2,1},{6... | collective-permute-start | bytes 1228808 | tf_op jit(solution)/shard_map/ppermute | solution.py:488
  16.0 12.6 %collective-permute-start.3 = (bf16[4,5,80,128]{3,2,1,0:T(8,128)(2,1)S(1)}, bf16[4,5,80,128]{3,2,1,0:T(8,128)(2,1)S(1)}, u32[]{:S(2)}, u32[]{:S(2)}) collective-permute-start(bf16[4,5,80,128]{3,2,1,0:T(8,128)(2,1)S(1)} %get-tuple-element.18.q_own_ref), channel_id=1, source_target_pairs={{1,0},{5,4},{9,8},{13,12},{17,16},{21,20},{25,24},{29,28},{0,1},{4... | collective-permute-start | bytes 1228808 | tf_op jit(solution)/shard_map/ppermute | solution.py:489
